TPU v7x, 128 devices: a whole 4x4x4 slice. The times are simulated.
128 devices in a mesh: region: 8 (over y, core), sub: 16 (over x, z).
Axes of the slice: x: 4, y: 4, z: 4, core: 2. Of those that a mesh axis runs over, the one named last changes fastest.
Arguments:
- orbitals: bfloat16 [512, 48, 2304], P(('region', 'sub')), may hold values from -6 to 6
- trial_set: bfloat16 [512, 48, 2304], P(('region', 'sub')), may hold values from -6 to 6
- own_slot: int32 [512], P(('region', 'sub')), may hold values from 0 to 3
- partner_route: int32 [512, 1], P(('region', 'sub')), may hold values from 0 to 16; in each aligned block of 4 rows (0 to 3, 4 to 7, ...) at most 2 rows name the same one
- partner_slot: int32 [512], P(('region', 'sub')), may hold values from 0 to 3
- offsets: int32 [512, 3], replicated, may hold values from 0 to 23
Outputs:
- fock_orbitals: bfloat16 [512, 48, 2304], P(('region', 'sub'))
- fock_trial: bfloat16 [512, 48, 2304], P(('region', 'sub'))
Inputs may be any that keep to these rules, and one draw needn't show every extreme that they name: `partner_route`: values below 16 name the device of the same region with that sub index; 16 names the device of the next region (after the last comes the first) with the same sub index. Among the 4 pairs of one device no value occurs more than 2 times, and some device has a value exactly 2 times.
All inputs are finite; a program needn't handle non-finite values.
Results may differ from a plain program's by a relative error of at most 0.0042.
Values may be sent and summed in bfloat16 or wider, within the bound.
No kernel may reach another device: no remote copies, remote signals or barrier semaphores. Data moves between devices by JAX's collectives and lax.ppermute only.
A program may use at most 192 MiB of HBM per device.

v0:
```python
import math

import jax
import jax.numpy as jnp
import ml_dtypes
import numpy as np
from jax import lax
from jax.experimental import pallas as pl
from jax.experimental.pallas import tpu as pltpu
from jax.sharding import PartitionSpec as P

BOX = 48
PLANE = BOX * BOX
CHUNK = PLANE // 6
SCREEN = 0.5
GRID = 4
N_SUB = GRID * GRID
ORB_DEV = 4
PAIRS_DEV = 4
N_PAIRS = N_SUB * PAIRS_DEV

PLACES = ((0, 0), (0, 1), (1, 0), (1, 1), (1, 3), (3, 1))
REGION_SOURCE = len(PLACES)
SOURCES = len(PLACES) + 1
LIST_WIDTH = 16
TASK_WIDTH = 8
LISTED = PAIRS_DEV * LIST_WIDTH
NOTE_ROWS = 16
SET_ROWS = ORB_DEV * BOX
SIZES = (4, 4, 4, 2, 2, 4, 4, 4)
N_OUT = len(SIZES)
N_TABLES = 4
BLOCKS_Y = 6
BLOCKS_Z = 3
MARGIN = 24
ROWS_PADDED = BOX + 2 * MARGIN
SIDE_Y = 3
SIDE_Z = 2
WIDE_Y = BLOCKS_Y + 2 * SIDE_Y
WIDE_Z = BLOCKS_Z + 2 * SIDE_Z
MAX_TASKS = 2 * len(PLACES) * PAIRS_DEV
HALF_ROOT3 = math.sqrt(3.0) / 2.0
F32 = jnp.float32
BF16 = jnp.bfloat16


def meeting_table():
    found = [[] for _ in range(N_SUB)]
    for i, (ax, az) in enumerate(PLACES):
        for j, (bx, bz) in enumerate(PLACES):
            delta = (ax - bx) % GRID * GRID + (az - bz) % GRID
            found[delta].append(i + 8 * j)
    most = max(len(f) for f in found)
    codes = np.array([f + [f[-1]] * (most - len(f)) for f in found], np.int32)
    counts = np.array([len(f) for f in found], np.int32)
    return np.concatenate([counts, codes.reshape(-1)]), most


def high_low(matrix):
    high = matrix.astype(ml_dtypes.bfloat16)
    low = (matrix - high.astype(np.float64)).astype(ml_dtypes.bfloat16)
    return np.stack([high, low])


def cas(angles):
    return np.cos(angles) + np.sin(angles)


def transform_tables():
    turn = 2.0 * math.pi / BOX
    n = np.arange(BOX)
    line = cas(turn * (n[:, None] * n[None, :] % BOX))
    q, w = np.arange(8), np.arange(16)

    def angle_y(j):
        return turn * (q[:, None] * (6 * q[None, :] + j) % BOX)

    def angle_z(j):
        return turn * (w[:, None] * (3 * w[None, :] + j) % BOX)

    def both_parts(angle):
        c, s = np.cos(angle), np.sin(angle)
        return np.block([[c, -s], [s, c]])

    def planes(y, z, sign):
        whole = angle_y(y)[:, None, :, None] + sign * angle_z(z)[None, :, None, :]
        return both_parts(whole.reshape(128, 128))

    def real_complex(y):
        z = both_parts(angle_z(1)).reshape(2, 16, 2, 16)
        return np.einsum("qm,awbn->aqwbmn", cas(angle_y(y)), z).reshape(256, 256)

    def complex_real(y):
        return np.kron(both_parts(angle_y(y)), cas(angle_z(0)))

    zero = np.zeros((128, 128))
    real = [np.kron(cas(angle_y(y)), cas(angle_z(0))) for y in (0, 3)]
    waves = [np.block([[real[0], zero], [zero, real[1]]]), real_complex(0), real_complex(3)]
    waves += [complex_real(1), complex_real(2)]
    for y in (1, 2):
        waves += [planes(y, 1, 1), planes(y, 1, -1)]
    waves = np.stack(waves)
    lam = 4.0 * np.sin(math.pi * n / BOX) ** 2

    def spectrum(y, z, weight):
        ky, kz = 6 * q + y, 3 * w + z
        total = lam[:, None, None] + lam[ky][None, :, None] + lam[kz][None, None, :] + SCREEN
        return (weight * 4.0 * math.pi / total / float(BOX**3)).reshape(BOX, 128)

    order = [(0, 0, 1.0), (3, 0, 1.0)]
    for y, z in ((0, 1), (3, 1), (1, 0), (2, 0), (1, 1), (1, 1), (2, 1), (2, 1)):
        order += [(y, z, 2.0)] * 2
    green = np.concatenate([spectrum(*o) for o in order], axis=1)
    rows = high_low(line)
    rows = np.block([[rows[0], rows[0]], [rows[1], np.zeros_like(rows[1])]])
    return dict(
        waves=high_low(waves),
        waves_back=high_low(waves.transpose(0, 2, 1)),
        green=green.astype(np.float32),
        rows=rows,
    )


TABLES = ("waves", "waves_back", "green", "rows")


def order_table():
    lane = np.arange(8 * BOX)
    q, c, w = lane // BOX, lane % BOX // 16, lane % 16
    table = np.zeros((8 * BOX, 8 * BOX), np.float32)
    table[lane, c * 128 + q * 16 + w] = 1.0
    return table.astype(ml_dtypes.bfloat16)


def plan_kernel(most, where, meta, offsets, table, chosen, used):
    region, sub, n_region = where[0], where[1], where[2]
    sign = 1 - 2 * (region & 1)
    next_region = jnp.where(region + 1 == n_region, 0, region + 1)
    for i in range(2 * len(PLACES)):
        used[i] = 0

    def place(pair, turn):
        own_slot = meta[pair]
        route = meta[PAIRS_DEV + pair]
        partner_slot = meta[2 * PAIRS_DEV + pair]
        abroad = route == N_SUB
        other = jnp.where(abroad, sub, route)
        dx = (sign * ((other >> 2) - (sub >> 2))) & 3
        dz = (sign * ((other & 3) - (sub & 3))) & 3
        delta = dx * GRID + dz
        count = jnp.where(abroad, 1, table[delta])

        @pl.when(jnp.where(count == 1, 0, 1) == turn)
        def _():
            row = pair * LIST_WIDTH
            for kind in range(3):
                load_of = len(PLACES) * min(kind, 1)
                best_load = jnp.int32(1 << 20)
                best_code = jnp.int32(0)
                for k in range(most):
                    code = table[N_SUB + delta * most + k]
                    load = used[load_of + (code & 7)]
                    better = load < best_load
                    best_load = jnp.where(better, load, best_load)
                    best_code = jnp.where(better, code, best_code)
                at = jnp.where(abroad, 0, best_code & 7)
                used[load_of + at] = used[load_of + at] + 1
                chosen[row + 2 * kind] = at
                chosen[row + 2 * kind + 1] = jnp.where(
                    abroad, REGION_SOURCE, (best_code >> 3) & 7
                )
            first = (region * N_SUB + sub) * ORB_DEV + own_slot
            second_region = jnp.where(abroad, next_region, region)
            second = (second_region * N_SUB + other) * ORB_DEV + partner_slot
            chosen[row + 6] = own_slot
            chosen[row + 7] = partner_slot
            for c in range(3):
                chosen[row + 8 + c] = offsets[first * 3 + c] - offsets[second * 3 + c]
            for c in range(11, LIST_WIDTH):
                chosen[row + c] = 0

    for turn in range(2):
        for pair in range(PAIRS_DEV):
            place(pair, turn)


def three_dots(high, low, weights, index):
    boxes_high = jnp.concatenate([high, low], axis=0)
    half = high.shape[0]
    wide = jnp.dot(boxes_high, weights[0, index], preferred_element_type=F32)
    rest = jnp.dot(high, weights[1, index], preferred_element_type=F32)
    return wide[:half] + wide[half:] + rest


def split(value):
    high = value.astype(BF16)
    return high, (value - high.astype(F32)).astype(BF16)


def six_points(x):
    u = [x[r] + x[r + 3] for r in range(3)]
    v = [x[r] - x[r + 3] for r in range(3)]
    return (
        u[0] + u[1] + u[2],
        v[0] - v[1] + v[2],
        v[0] + 0.5 * (v[1] - v[2]),
        -HALF_ROOT3 * (v[1] + v[2]),
        u[0] - 0.5 * (u[1] + u[2]),
        -HALF_ROOT3 * (u[1] - u[2]),
    )


def six_points_back(t0, t3, t1r, t1i, t2r, t2i):
    a0 = t0 + t2r
    t2h = t0 - 0.5 * t2r
    t2s = HALF_ROOT3 * t2i
    a1 = t2h - t2s
    a2 = t2h + t2s
    t1s = HALF_ROOT3 * t1i
    b0 = t3 + t1r
    b1 = 0.5 * t1r - t3 - t1s
    b2 = t3 - 0.5 * t1r - t1s
    return a0 + b0, a1 + b1, a2 + b2, a0 - b0, a1 - b1, a2 - b2


def three_points(x):
    total = x[1] + x[2]
    return x[0] + total, x[0] - 0.5 * total, -HALF_ROOT3 * (x[1] - x[2])


def three_points_back(s0, s1r, s1i):
    low = s0 - 0.5 * s1r
    turned = HALF_ROOT3 * s1i
    return s0 + s1r, low - turned, low + turned


def solve(density, both, work, waves, waves_back, green, rows, boxes):
    for b in range(boxes):
        for g in range(BOX // 16):
            some = pl.ds(b * BOX + g * 16, 16)
            low_some = pl.ds((boxes + b) * BOX + g * 16, 16)
            columns = []
            for c in range(BLOCKS_Z):
                x = [density(b, pl.ds(g * 16, 16), r, c) for r in range(BLOCKS_Y)]
                columns.append(six_points(x))
            t = [three_points([columns[c][j] for c in range(BLOCKS_Z)]) for j in range(6)]
            parts = [t[0][0], t[1][0], t[0][1], t[0][2], t[1][1], t[1][2]]
            parts += [t[2][0], t[3][0], t[4][0], t[5][0]]
            for j in (2, 4):
                (_, rr, ri), (_, ir, ii) = t[j], t[j + 1]
                parts += [rr - ii, ri + ir, rr + ii, ir - ri]
            for i, part in enumerate(parts):
                high, low = split(part)
                both[some, pl.ds(i * 128, 128)] = high
                both[low_some, pl.ds(i * 128, 128)] = low

    def row_pass(value):
        stacked = jnp.concatenate(split(value), axis=0)
        result = jnp.dot(rows[...], stacked, preferred_element_type=F32)
        return result[:BOX] + result[BOX:]

    def plane_pass(weights):
        for group in range(9):
            lanes = pl.ds(group * 256, 256)
            high = both[pl.ds(0, boxes * BOX), lanes]
            low = both[pl.ds(boxes * BOX, boxes * BOX), lanes]
            work[:, lanes] = three_dots(high, low, weights, group)

    places = [
        (pl.ds(b * BOX, BOX), pl.ds((boxes + b) * BOX, BOX), pl.ds(group * 256, 256))
        for b in range(boxes)
        for group in range(9)
    ]
    plane_pass(waves)
    for some, _, lanes in places:
        work[some, lanes] = row_pass(work[some, lanes]) * green[:, lanes]
    for some, low_some, lanes in places:
        both[some, lanes], both[low_some, lanes] = split(row_pass(work[some, lanes]))
    plane_pass(waves_back)

    for b in range(boxes):
        for g in range(BOX // 16):
            some = pl.ds(b * BOX + g * 16, 16)
            p = [work[some, pl.ds(i * 128, 128)] for i in range(18)]
            t = [[p[0], p[2], p[3]], [p[1], p[4], p[5]]]
            for j in range(2):
                pr, pi, mr, mi = p[10 + 4 * j : 14 + 4 * j]
                t.append([p[6 + 2 * j], pr + mr, pi - mi])
                t.append([p[7 + 2 * j], pi + mi, mr - pr])
            t = [three_points_back(*parts) for parts in t]
            for c in range(BLOCKS_Z):
                values = six_points_back(*[t[j][c] for j in range(6)])
                for r, value in enumerate(values):
                    work[some, pl.ds((r * BLOCKS_Z + c) * 128, 128)] = value


def rounded(value):
    return value.astype(BF16).astype(F32)


def shift_box(padded, value, put, dx, dy, dz):
    for r in range(BLOCKS_Y):
        for c in range(BLOCKS_Z):
            at = ((r + SIDE_Y) * WIDE_Z + c + SIDE_Z) * ROWS_PADDED + MARGIN
            padded[pl.ds(at, BOX), :] = value(pl.ds((r * BLOCKS_Z + c) * 128, 128))
    fine_y, fine_z = dy & 7, dz & 15
    start = ((dy >> 3) + SIDE_Y) * WIDE_Z + (dz >> 4) + SIDE_Z
    base = start * ROWS_PADDED + MARGIN + dx
    lane = lax.broadcasted_iota(jnp.int32, (1, 128), 1)
    next_y = (lane >> 4) < fine_y
    next_z = (lane & 15) < fine_z
    carried = (lane & 15) + fine_z >= 16
    ahead = fine_y * 16 + fine_z
    turn = (128 - ahead) & 127
    turn_carried = (128 + 16 - ahead) & 127

    def block(r, c):
        return padded[pl.ds(base + (r * WIDE_Z + c) * ROWS_PADDED, BOX), :]

    for r in range(BLOCKS_Y):
        mixed = [jnp.where(next_y, block(r + 1, c), block(r, c)) for c in range(BLOCKS_Z + 1)]
        for c in range(BLOCKS_Z):
            source = jnp.where(next_z, mixed[c + 1], mixed[c])
            out = jnp.where(
                carried, pltpu.roll(source, turn_carried, 1), pltpu.roll(source, turn, 1)
            )
            put(pl.ds((r * BLOCKS_Z + c) * 128, 128), out)


def exchange_kernel(part, *refs):
    second = part > 0
    sets = 2 if second else 1
    carried = N_OUT if part == 2 else 0
    n_in = sets * (SOURCES + 1)
    listing, *refs = refs
    boxes_in, refs = refs[:n_in], refs[n_in:]
    tables_in, refs = refs[:N_TABLES], refs[N_TABLES:]
    sums_in, refs = refs[:carried], refs[carried:]
    outs, refs = refs[:N_OUT], refs[N_OUT:]
    tables, refs = refs[:N_TABLES], refs[N_TABLES:]
    acc, stage, held, theirs, both, work, padded, mine, sems, table_sems, out_sems = refs

    mine[0] = 0
    for home in range(len(PLACES)):

        def check(pair, carry, home=home):
            row = (home * PAIRS_DEV + pair) * LIST_WIDTH
            for kind in (1, 2) if second else (0,):

                @pl.when(listing[row + 2 * kind] == home)
                def _(kind=kind):
                    at = mine[0]
                    mine[0] = at + 1
                    task = (at + 1) * TASK_WIDTH
                    mine[task] = home
                    mine[task + 1] = listing[row + 2 * kind + 1]
                    for c in range(5):
                        mine[task + 2 + c] = listing[row + 6 + c]
                    mine[task + 7] = kind

            return carry

        lax.fori_loop(0, PAIRS_DEV, check, 0)

    count = mine[0]
    steps = (count + 1) >> 1
    half = (steps + 1) >> 1
    begin = half if part == 2 else 0
    end = half if part == 1 else steps

    def table_copies():
        return [
            pltpu.make_async_copy(tables_in[i], tables[i], table_sems.at[i])
            for i in range(N_TABLES)
        ]

    def fetch(group, source, slot, target, sem):
        refs_of = boxes_in[group * (SOURCES + 1) : (group + 1) * (SOURCES + 1)]

        def start(ref, row):
            row = pl.multiple_of(row, 16)
            pltpu.make_async_copy(ref.at[pl.ds(row, BOX)], target, sem).start()

        for s in range(SOURCES):
            if s == 3:
                for part_of in range(2):

                    @pl.when((source == s) & ((slot >> 1) == part_of))
                    def _(part_of=part_of):
                        start(refs_of[3 + part_of], (slot & 1) * BOX)
            else:
                at = s if s < 3 else s + 1

                @pl.when(source == s)
                def _(at=at):
                    start(refs_of[at], slot * BOX)

    def each_load(step, act):
        for i in range(2):
            task = (step * 2 + i + 1) * TASK_WIDTH

            @pl.when(step * 2 + i < count)
            def _(i=i, task=task):
                kind = mine[task + 7]
                act(kind == 1, mine[task], mine[task + 2], 2 * i)
                act(kind == 2, mine[task + 1], mine[task + 3], 2 * i + 1)

    def start_loads(step, buffer):
        def act(of_trial, source, slot, i):
            if second:

                @pl.when(of_trial)
                def _():
                    fetch(1, source, slot, held.at[buffer, i], sems.at[buffer, i])

                @pl.when(jnp.logical_not(of_trial))
                def _():
                    fetch(0, source, slot, held.at[buffer, i], sems.at[buffer, i])
            else:
                fetch(0, source, slot, held.at[buffer, i], sems.at[buffer, i])

        each_load(step, act)

    def wait_loads(step, buffer):
        def act(of_trial, source, slot, i):
            pltpu.make_async_copy(
                boxes_in[0].at[pl.ds(0, BOX)], held.at[buffer, i], sems.at[buffer, i]
            ).wait()

        each_load(step, act)

    def sum_copies(into):
        copies = []
        for i, size in enumerate(SIZES):
            low = sum(SIZES[:i]) * BOX
            vmem = stage.at[pl.ds(low, size * BOX)]
            if into:
                copies.append(pltpu.make_async_copy(sums_in[i], vmem, out_sems.at[i]))
            else:
                copies.append(pltpu.make_async_copy(vmem, outs[i], out_sems.at[i]))
        return copies

    @pl.when(begin < end)
    def _():
        start_loads(begin, begin & 1)
        for copy in table_copies():
            copy.start()

    if carried:
        for copy in sum_copies(True):
            copy.start()
    padded[...] = jnp.zeros(padded.shape, F32)

    def box_rows(i):
        return pl.ds(pl.multiple_of(i * BOX, BOX), BOX)

    if carried:
        for copy in sum_copies(True):
            copy.wait()

    def prepare(i, carry):
        if carried:
            acc[box_rows(i), :] = stage[box_rows(i), :].astype(F32)
        else:
            acc[box_rows(i), :] = jnp.zeros((BOX, PLANE), F32)
        return carry

    lax.fori_loop(0, SOURCES * ORB_DEV, prepare, 0)

    def add(source, slot, lanes, value):
        at = box_rows(source * ORB_DEV + slot)
        acc[at, lanes] = acc[at, lanes] + value

    def one_step(step, carry):
        buffer = step & 1

        @pl.when(step + 1 < end)
        def _():
            start_loads(step + 1, 1 - buffer)

        wait_loads(step, buffer)
        for i in range(2):
            task = (step * 2 + i + 1) * TASK_WIDTH

            @pl.when(step * 2 + i < count)
            def _(i=i, task=task):
                def value(lanes):
                    return held[buffer, 2 * i + 1, :, lanes].astype(F32)

                def put(lanes, block):
                    theirs[i, :, lanes] = block

                shift_box(padded, value, put, mine[task + 4], mine[task + 5], mine[task + 6])

        @pl.when(step == begin)
        def _():
            for copy in table_copies():
                copy.wait()

        def density(b, some, r, c):
            lanes = pl.ds((r * BLOCKS_Z + c) * 128, 128)
            return held[buffer, 2 * b, some, lanes].astype(F32) * theirs[b, some, lanes]

        solve(density, both, work, *tables, 2)
        for i in range(2):
            task = (step * 2 + i + 1) * TASK_WIDTH
            there = step * 2 + i < count
            kind = mine[task + 7]

            @pl.when(there & (kind != 2))
            def _(i=i, task=task):
                near = rounded(work[pl.ds(i * BOX, BOX), :] * theirs[i])
                add(mine[task], mine[task + 2], pl.ds(0, PLANE), near)

            @pl.when(there & (kind != 1))
            def _(i=i, task=task):
                def value(lanes):
                    mine_box = held[buffer, 2 * i, :, lanes].astype(F32)
                    return rounded(work[pl.ds(i * BOX, BOX), lanes] * mine_box)

                def put(lanes, block):
                    add(mine[task + 1], mine[task + 3], lanes, block)

                shift_box(padded, value, put, -mine[task + 4], -mine[task + 5], -mine[task + 6])

        return carry

    lax.fori_loop(begin, end, one_step, 0)

    copies = sum_copies(False)
    at = 0
    for copy, size in zip(copies, SIZES):

        def put(i, carry):
            stage[box_rows(i), :] = acc[box_rows(i), :].astype(BF16)
            return carry

        lax.fori_loop(at, at + size, put, 0)
        copy.start()
        at += size
    for copy in copies:
        copy.wait()


def exchange(part, listing, boxes, tables, sums=()):
    any_space = pl.BlockSpec(memory_space=pl.ANY)
    smem = pl.BlockSpec(memory_space=pltpu.SMEM)
    outs = [
        jax.ShapeDtypeStruct((size * BOX, PLANE), BF16) for size in SIZES
    ]

    def kernel(*refs):
        exchange_kernel(part, *refs)

    return pl.pallas_call(
        kernel,
        out_shape=outs,
        in_specs=[smem] + [any_space] * (len(boxes) + len(tables) + len(sums)),
        out_specs=[any_space] * len(outs),
        scratch_shapes=[
            *[pltpu.VMEM(t.shape, t.dtype) for t in tables],
            pltpu.VMEM((SOURCES * ORB_DEV * BOX, PLANE), F32),
            pltpu.VMEM((SOURCES * ORB_DEV * BOX, PLANE), BF16),
            pltpu.VMEM((2, 4, BOX, PLANE), BF16),
            pltpu.VMEM((2, BOX, PLANE), F32),
            pltpu.VMEM((4 * BOX, PLANE), BF16),
            pltpu.VMEM((2 * BOX, PLANE), F32),
            pltpu.VMEM((WIDE_Y * WIDE_Z * ROWS_PADDED, 128), F32),
            pltpu.SMEM(((MAX_TASKS + 3) * TASK_WIDTH,), jnp.int32),
            pltpu.SemaphoreType.DMA((2, 4)),
            pltpu.SemaphoreType.DMA((N_TABLES,)),
            pltpu.SemaphoreType.DMA((N_OUT,)),
        ],
        compiler_params=pltpu.CompilerParams(vmem_limit_bytes=56 * 1024 * 1024),
        cost_estimate=pl.CostEstimate(
            flops=10_000_000_000, bytes_accessed=30_000_000, transcendentals=0
        ),
        name=("first_application", "second_early", "second_late")[part],
    )(listing, *boxes, *tables, *sums)


def reorder_kernel(with_notes, box, *refs):
    order, out = refs[-2:]
    for r in range(BLOCKS_Y):
        lanes = pl.ds(r * CHUNK, CHUNK)
        moved = jnp.dot(box[:, lanes], order[...], preferred_element_type=F32)
        out[pl.ds(0, SET_ROWS), lanes] = moved.astype(BF16)
    if with_notes:
        out[pl.ds(SET_ROWS, NOTE_ROWS), :] = refs[0][...]


def reorder(boxes, order, notes=()):
    rows = SET_ROWS + NOTE_ROWS * len(notes)

    def kernel(*refs):
        reorder_kernel(bool(notes), *refs)

    return pl.pallas_call(
        kernel,
        out_shape=jax.ShapeDtypeStruct((rows, PLANE), BF16),
        name="reorder",
        compiler_params=pltpu.CompilerParams(vmem_limit_bytes=32 * 1024 * 1024),
    )(boxes, *notes, order)


def total_kernel(*refs):
    *parts, order, out = refs
    for r in range(BLOCKS_Y):
        lanes = pl.ds(r * CHUNK, CHUNK)
        result = parts[0][:, lanes].astype(F32)
        for part in parts[1:]:
            result += part[:, lanes].astype(F32)
        moved = jnp.dot((-result).astype(BF16), order[...], preferred_element_type=F32)
        out[:, lanes] = moved.astype(BF16)


def total(parts, order):
    half = SET_ROWS // 2
    whole = pl.BlockSpec((CHUNK, CHUNK), lambda i: (0, 0))
    some = pl.BlockSpec((half, PLANE), lambda i: (i, 0))
    return pl.pallas_call(
        total_kernel,
        grid=(2,),
        out_shape=jax.ShapeDtypeStruct((SET_ROWS, PLANE), BF16),
        in_specs=[some] * len(parts) + [whole],
        out_specs=some,
        name="total",
        compiler_params=pltpu.CompilerParams(vmem_limit_bytes=32 * 1024 * 1024),
    )(*parts, order)


def moves(n_region):
    def step(dx, dz):
        pairs = []
        for region in range(n_region):
            sign = 1 - 2 * (region % 2)
            for x in range(GRID):
                for z in range(GRID):
                    to = (x + sign * dx) % GRID * GRID + (z + sign * dz) % GRID
                    pairs.append((region * N_SUB + x * GRID + z, region * N_SUB + to))

        def move(block):
            return lax.ppermute(block, ("region", "sub"), pairs)

        return move

    def across(distance):
        pairs = [(i, (i + distance) % n_region) for i in range(n_region)]

        def move(block):
            return lax.ppermute(block, "region", pairs)

        return move

    return step, across


def per_device(orbitals, trial_set, own_slot, partner_route, partner_slot, offsets):
    n_region = lax.axis_size("region")
    region = lax.axis_index("region")
    sub = lax.axis_index("sub")
    step, across = moves(n_region)
    tables = transform_tables()
    tables = [
        jnp.asarray(tables[k])
        for k in TABLES
    ]
    order, order_back = jnp.asarray(order_table()), jnp.asarray(order_table().T.copy())
    table, most = meeting_table()
    meta = jnp.concatenate([own_slot, partner_route[:, 0], partner_slot])
    where = jnp.stack([region, sub, jnp.int32(n_region)]).astype(jnp.int32)
    smem = pl.BlockSpec(memory_space=pltpu.SMEM)

    def planner(*refs):
        plan_kernel(most, *refs)

    chosen = pl.pallas_call(
        planner,
        out_shape=jax.ShapeDtypeStruct((LISTED,), jnp.int32),
        in_specs=[smem] * 4,
        out_specs=smem,
        scratch_shapes=[pltpu.SMEM((2 * len(PLACES),), jnp.int32)],
        name="plan",
    )(where, meta, offsets.reshape(-1), jnp.asarray(table))

    def near_places(boxes):
        return step(0, 1)(boxes), step(1, 0)(boxes), across(-1)(boxes)

    def cut(b01, b10):
        return b01[: 2 * BOX], b10[2 * BOX :]

    def far_places(b01, b10, halves):
        low, high = halves
        return step(1, 0)(low), step(0, 1)(high), step(0, -1)(b10), step(-1, 0)(b01)

    def begin_back(parts):
        own, c01, c10, c11_low, c11_high, c13, c31, c_abroad = parts
        return (
            step(0, 1)(c13),
            step(1, 0)(c31),
            step(-1, 0)(c11_low),
            step(0, -1)(c11_high),
            across(1)(c_abroad),
        )

    def merge(parts, arrived):
        r13, r31, r11_low, r11_high, _ = arrived
        none = jnp.zeros_like(r11_low)
        low = jnp.concatenate([r11_low, none])
        high = jnp.concatenate([none, r11_high])
        m01 = (parts[1].astype(F32) + r31.astype(F32) + low.astype(F32)).astype(BF16)
        m10 = (parts[2].astype(F32) + r13.astype(F32) + high.astype(F32)).astype(BF16)
        return step(0, -1)(m01), step(-1, 0)(m10)

    def finish(parts, arrived, merged):
        result = total([parts[0], arrived[4], *merged], order_back)
        return result.reshape(ORB_DEV, BOX, PLANE)

    ordered = lax.optimization_barrier
    notes = jnp.pad(chosen.astype(BF16)[None], ((0, NOTE_ROWS - 1), (0, PLANE - LISTED)))
    trials = reorder(trial_set.reshape(SET_ROWS, PLANE), order)
    boxes = reorder(orbitals.reshape(SET_ROWS, PLANE), order, (notes,))
    t01, t10, t_abroad = near_places(trials)
    boxes, t01, t10, t_abroad = ordered((boxes, t01, t10, t_abroad))
    t_cut = cut(t01, t10)
    o01, o10, o_abroad = near_places(boxes)
    o01, o10, o_abroad, t_cut = ordered((o01, o10, o_abroad, t_cut))
    o_far = far_places(o01, o10, cut(o01, o10))
    t01, t10, t_cut, o_far = ordered((t01, t10, t_cut, o_far))
    t_far = far_places(t01, t10, t_cut)
    orbital_boxes = [boxes, o01, o10, *o_far, o_abroad]
    notes = [boxes, o01, o10, o_far[1], o_far[2], o_far[3]]
    listing = jnp.concatenate([n[-NOTE_ROWS, :LISTED] for n in notes]).astype(jnp.int32)
    first = exchange(0, listing, orbital_boxes, tables)
    arrived_first = begin_back(first)
    first, listing, t_far = ordered((first, listing, t_far))
    all_boxes = orbital_boxes + [trials, t01, t10, *t_far, t_abroad]
    early = exchange(1, listing, all_boxes, tables)
    early, first, arrived_first = ordered((early, first, arrived_first))
    merged_first = merge(first, arrived_first)
    late = exchange(2, listing, all_boxes, tables, early)
    late, merged_first = ordered((late, merged_first))
    result_first = finish(first, arrived_first, merged_first)
    arrived_late = begin_back(late)
    result_second = finish(late, arrived_late, merge(late, arrived_late))
    return result_first, result_second


def solution(mesh):
    in_specs = (
        P(("region", "sub"), None, None),
        P(("region", "sub"), None, None),
        P(("region", "sub")),
        P(("region", "sub"), None),
        P(("region", "sub")),
        P(),
    )
    out_specs = (P(("region", "sub"), None, None), P(("region", "sub"), None, None))
    return jax.shard_map(
        per_device, mesh=mesh, in_specs=in_specs, out_specs=out_specs, check_vma=False
    )
```

profile of v0, /device:TPU:8, one launch (start us, length us, event | category | flops | bytes accessed | tf_op | source)
XLA Modules:
  0.0 163.6 jit_solution(9423428080562778216)
XLA Ops:
  0.7 1.0 copy-done.1
  1.6 1.2 copy-done.7
  2.8 0.7 reorder.3.refs_9_
  3.5 2.0 %collective-permute-start = (bf16[192,2304]{1,0:T(8,128)(2,1)S(1)}, bf16[192,2304]{1,0:T(8,128)(2,1)}, u32[]{:S(2)}, u32[]{:S(2)}) collective-permute-start(bf16[192,2304]{1,0:T(8,128)(2,1)S(1)} %reorder.3.refs_9_), channel_id=1, source_target_pairs={{0,1},{1,2},{2,3},{3,0},{4,5},{5,6},{6,7},{7,4},{8,9},{9,10},{10,1... | collective-permute-start | bytes 2654216 | tf_op jit(solution)/shard_map/ppermute | solution.py:643
  5.5 1.5 collective-permute-start.1
  7.0 2.7 %collective-permute-start.2 = (bf16[192,2304]{1,0:T(8,128)(2,1)S(1)}, bf16[192,2304]{1,0:T(8,128)(2,1)S(1)}, u32[]{:S(2)}, u32[]{:S(2)}) collective-permute-start(bf16[192,2304]{1,0:T(8,128)(2,1)S(1)} %reorder.3.refs_9_), channel_id=1, source_target_pairs={{0,112},{16,0},{32,16},{48,32},{64,48},{80,64},{96,80},{112,96},{1... | collective-permute-start | bytes 2654216 | tf_op jit(solution)/shard_map/ppermute | solution.py:651
  9.9 0.8 reshape.20.refs_2_
  11.9 1.7 %plan.1 = s32[64]{0:T(128)} custom-call(s32[3]{0:T(128)} %pad_add_fusion.refs_0_, s32[12]{0:T(128)} %pad_add_fusion.1.refs_1_, s32[1536]{0:T(1024)} %reshape.20.refs_2_, s32[112]{0:T(128)} %constant.35.clone.refs_3_), custom_call_target="tpu_custom_call" | custom-call | tf_op jit(solution)/shard_map/plan/pallas_call | solution.py:677
  13.6 0.6 convert_bitcast_fusion
  14.2 0.7 reorder.2.refs_1_
  14.9 3.9 %collective-permute-done.refs_10_ = bf16[192,2304]{1,0:T(8,128)(2,1)} collective-permute-done((bf16[192,2304]{1,0:T(8,128)(2,1)S(1)}, bf16[192,2304]{1,0:T(8,128)(2,1)}, u32[]{:S(2)}, u32[]{:S(2)}) %collective-permute-start) | collective-permute-done | bytes 884768 | tf_op jit(solution)/shard_map/ppermute | solution.py:643
  18.8 1.1 collective-permute-done.1.refs_11_
  20.3 1.5 collective-permute-start.3
  22.1 1.2 collective-permute-start.5
  23.2 1.0 slice.31
  24.3 1.0 slice.32
  25.4 10.0 %collective-permute-done.3.refs_2_ = bf16[208,2304]{1,0:T(8,128)(2,1)S(1)} collective-permute-done((bf16[208,2304]{1,0:T(8,128)(2,1)S(1)}, bf16[208,2304]{1,0:T(8,128)(2,1)S(1)}, u32[]{:S(2)}, u32[]{:S(2)}) %collective-permute-start.3) | collective-permute-done | bytes 958496 | tf_op jit(solution)/shard_map/ppermute | solution.py:643
  35.3 1.5 collective-permute-done.4.refs_3_
  36.9 1.8 %collective-permute-start.8 = (bf16[208,2304]{1,0:T(8,128)(2,1)S(1)}, bf16[208,2304]{1,0:T(8,128)(2,1)S(1)}, u32[]{:S(2)}, u32[]{:S(2)}) collective-permute-start(bf16[208,2304]{1,0:T(8,128)(2,1)S(1)} %collective-permute-done.4.refs_3_), channel_id=1, source_target_pairs={{0,3},{1,0},{2,1},{3,2},{4,7},{5,4},{6,5},{7,6},{8,11},{9,8},{10,9... | collective-permute-start | bytes 2875400 | tf_op jit(solution)/shard_map/ppermute | solution.py:643
  38.8 1.1 collective-permute-start.7
  40.0 1.8 %collective-permute-start.6 = (bf16[96,2304]{1,0:T(8,128)(2,1)S(1)}, bf16[96,2304]{1,0:T(8,128)(2,1)S(1)}, u32[]{:S(2)}, u32[]{:S(2)}) collective-permute-start(bf16[96,2304]{1,0:T(8,128)(2,1)S(1)} %slice.35), channel_id=1, source_target_pairs={{0,4},{1,5},{2,6},{3,7},{4,8},{5,9},{6,10},{7,11},{8,12},{9,13},{1... | collective-permute-start | bytes 1327112 | tf_op jit(solution)/shard_map/ppermute | solution.py:643
  41.7 12.6 %collective-permute-done.6.refs_4_ = bf16[96,2304]{1,0:T(8,128)(2,1)S(1)} collective-permute-done((bf16[96,2304]{1,0:T(8,128)(2,1)S(1)}, bf16[96,2304]{1,0:T(8,128)(2,1)S(1)}, u32[]{:S(2)}, u32[]{:S(2)}) %collective-permute-start.6) | collective-permute-done | bytes 442400 | tf_op jit(solution)/shard_map/ppermute | solution.py:643
  54.8 1.5 collective-permute-done.8.refs_6_
  56.3 0.9 collective-permute-done.9.refs_7_
  57.4 0.7 convert_element_type.57.refs_0_
  58.1 2.1 %collective-permute-start.12 = (bf16[192,2304]{1,0:T(8,128)(2,1)}, bf16[192,2304]{1,0:T(8,128)(2,1)S(1)}, u32[]{:S(2)}, u32[]{:S(2)}) collective-permute-start(bf16[192,2304]{1,0:T(8,128)(2,1)} %collective-permute-done.1.refs_11_), channel_id=1, source_target_pairs={{0,3},{1,0},{2,1},{3,2},{4,7},{5,4},{6,5},{7,6},{8,11},{9,8},{10,9... | collective-permute-start | bytes 2654216 | tf_op jit(solution)/shard_map/ppermute | solution.py:643
  60.4 1.8 %collective-permute-start.10 = (bf16[96,2304]{1,0:T(8,128)(2,1)S(1)}, bf16[96,2304]{1,0:T(8,128)(2,1)S(1)}, u32[]{:S(2)}, u32[]{:S(2)}) collective-permute-start(bf16[96,2304]{1,0:T(8,128)(2,1)S(1)} %slice.31), channel_id=1, source_target_pairs={{0,4},{1,5},{2,6},{3,7},{4,8},{5,9},{6,10},{7,11},{8,12},{9,13},{1... | collective-permute-start | bytes 1327112 | tf_op jit(solution)/shard_map/ppermute | solution.py:643
  62.2 12.7 %first_application.1 = (bf16[192,2304]{1,0:T(8,128)(2,1)}, bf16[192,2304]{1,0:T(8,128)(2,1)}, bf16[192,2304]{1,0:T(8,128)(2,1)}, bf16[96,2304]{1,0:T(8,128)(2,1)...) custom-call(s32[384]{0:T(512)} %convert_element_type.57.refs_0_, ...), custom_call_target="tpu_custom_call" | custom-call | flops 10000000000 | bytes 30000000 | tf_op jit(solution)/shard_map/first_application/pallas_call | solution.py:555
  75.0 2.6 %collective-permute-start.15 = (bf16[192,2304]{1,0:T(8,128)(2,1)}, bf16[192,2304]{1,0:T(8,128)(2,1)S(1)}, u32[]{:S(2)}, u32[]{:S(2)}) collective-permute-start(bf16[192,2304]{1,0:T(8,128)(2,1)} %get-tuple-element.95), channel_id=1, source_target_pairs={{0,4},{1,5},{2,6},{3,7},{4,8},{5,9},{6,10},{7,11},{8,12},{9,13},{1... | collective-permute-start | bytes 2654216 | tf_op jit(solution)/shard_map/ppermute | solution.py:643
  77.6 0.8 copy-done.27
  78.4 0.9 copy-done.22
  79.3 6.4 %collective-permute-start.16 = (bf16[96,2304]{1,0:T(8,128)(2,1)}, bf16[96,2304]{1,0:T(8,128)(2,1)S(1)}, u32[]{:S(2)}, u32[]{:S(2)}) collective-permute-start(bf16[96,2304]{1,0:T(8,128)(2,1)} %get-tuple-element.92), channel_id=1, source_target_pairs={{0,12},{1,13},{2,14},{3,15},{4,0},{5,1},{6,2},{7,3},{8,4},{9,5},{1... | collective-permute-start | bytes 1327112 | tf_op jit(solution)/shard_map/ppermute | solution.py:643
  85.8 3.2 %collective-permute-start.17 = (bf16[96,2304]{1,0:T(8,128)(2,1)}, bf16[96,2304]{1,0:T(8,128)(2,1)S(1)}, u32[]{:S(2)}, u32[]{:S(2)}) collective-permute-start(bf16[96,2304]{1,0:T(8,128)(2,1)} %get-tuple-element.93), channel_id=1, source_target_pairs={{0,3},{1,0},{2,1},{3,2},{4,7},{5,4},{6,5},{7,6},{8,11},{9,8},{10,9... | collective-permute-start | bytes 1327112 | tf_op jit(solution)/shard_map/ppermute | solution.py:643
  89.0 12.4 %second_early.1 = (bf16[192,2304]{1,0:T(8,128)(2,1)}, bf16[192,2304]{1,0:T(8,128)(2,1)}, bf16[192,2304]{1,0:T(8,128)(2,1)}, bf16[96,2304]{1,0:T(8,128)(2,1)}, bf...) custom-call(s32[384]{0:T(512)} %convert_element_type.57.refs_0_, ...), custom_call_target="tpu_custom_call" | custom-call | flops 10000000000 | bytes 30000000 | tf_op jit(solution)/shard_map/second_early/pallas_call | solution.py:555
  101.7 7.3 %collective-permute-start.20 = (bf16[192,2304]{1,0:T(8,128)(2,1)S(1)}, bf16[192,2304]{1,0:T(8,128)(2,1)S(1)}, u32[]{:S(2)}, u32[]{:S(2)}) collective-permute-start(bf16[192,2304]{1,0:T(8,128)(2,1)S(1)} %add_convert_fusion.2), channel_id=1, source_target_pairs={{0,12},{1,13},{2,14},{3,15},{4,0},{5,1},{6,2},{7,3},{8,4},{9,5},{1... | collective-permute-start | bytes 2654216 | tf_op jit(solution)/shard_map/ppermute | solution.py:643
  109.4 12.7 %second_late.1 = (bf16[192,2304]{1,0:T(8,128)(2,1)}, bf16[192,2304]{1,0:T(8,128)(2,1)}, bf16[192,2304]{1,0:T(8,128)(2,1)}, bf16[96,2304]{1,0:T(8,128)(2,1)}, bf1...) custom-call(s32[384]{0:T(512)} %convert_element_type.57.refs_0_, ...), custom_call_target="tpu_custom_call" | custom-call | flops 10000000000 | bytes 30000000 | tf_op jit(solution)/shard_map/second_late/pallas_call | solution.py:555
  122.1 4.1 %collective-permute-done.19.refs_2_ = bf16[192,2304]{1,0:T(8,128)(2,1)S(1)} collective-permute-done((bf16[192,2304]{1,0:T(8,128)(2,1)S(1)}, bf16[192,2304]{1,0:T(8,128)(2,1)S(1)}, u32[]{:S(2)}, u32[]{:S(2)}) %collective-permute-start.19) | collective-permute-done | bytes 884768 | tf_op jit(solution)/shard_map/ppermute | solution.py:643
  126.2 3.2 %collective-permute-start.26 = (bf16[96,2304]{1,0:T(8,128)(2,1)}, bf16[96,2304]{1,0:T(8,128)(2,1)S(1)}, u32[]{:S(2)}, u32[]{:S(2)}) collective-permute-start(bf16[96,2304]{1,0:T(8,128)(2,1)} %get-tuple-element.151), channel_id=1, source_target_pairs={{0,3},{1,0},{2,1},{3,2},{4,7},{5,4},{6,5},{7,6},{8,11},{9,8},{10,9... | collective-permute-start | bytes 1327112 | tf_op jit(solution)/shard_map/ppermute | solution.py:643
  129.4 3.2 %collective-permute-start.23 = (bf16[96,2304]{1,0:T(8,128)(2,1)}, bf16[96,2304]{1,0:T(8,128)(2,1)S(1)}, u32[]{:S(2)}, u32[]{:S(2)}) collective-permute-start(bf16[96,2304]{1,0:T(8,128)(2,1)} %get-tuple-element.148), channel_id=1, source_target_pairs={{0,12},{1,13},{2,14},{3,15},{4,0},{5,1},{6,2},{7,3},{8,4},{9,5},{1... | collective-permute-start | bytes 1327112 | tf_op jit(solution)/shard_map/ppermute | solution.py:643
  132.7 4.0 %collective-permute-done.26 = bf16[96,2304]{1,0:T(8,128)(2,1)S(1)} collective-permute-done((bf16[96,2304]{1,0:T(8,128)(2,1)}, bf16[96,2304]{1,0:T(8,128)(2,1)S(1)}, u32[]{:S(2)}, u32[]{:S(2)}) %collective-permute-start.26) | collective-permute-done | bytes 442400 | tf_op jit(solution)/shard_map/ppermute | solution.py:643
  136.6 4.0 %collective-permute-done.25 = bf16[192,2304]{1,0:T(8,128)(2,1)S(1)} collective-permute-done((bf16[192,2304]{1,0:T(8,128)(2,1)}, bf16[192,2304]{1,0:T(8,128)(2,1)S(1)}, u32[]{:S(2)}, u32[]{:S(2)}) %collective-permute-start.25) | collective-permute-done | bytes 884768 | tf_op jit(solution)/shard_map/ppermute | solution.py:643
  140.6 1.4 add_convert_fusion
  142.1 2.6 %collective-permute-start.27 = (bf16[192,2304]{1,0:T(8,128)(2,1)S(1)}, bf16[192,2304]{1,0:T(8,128)(2,1)S(1)}, u32[]{:S(2)}, u32[]{:S(2)}) collective-permute-start(bf16[192,2304]{1,0:T(8,128)(2,1)S(1)} %add_convert_fusion), channel_id=1, source_target_pairs={{0,12},{1,13},{2,14},{3,15},{4,0},{5,1},{6,2},{7,3},{8,4},{9,5},{1... | collective-permute-start | bytes 2654216 | tf_op jit(solution)/shard_map/ppermute | solution.py:643
  144.7 3.8 %collective-permute-done.22 = bf16[192,2304]{1,0:T(8,128)(2,1)S(1)} collective-permute-done((bf16[192,2304]{1,0:T(8,128)(2,1)}, bf16[192,2304]{1,0:T(8,128)(2,1)S(1)}, u32[]{:S(2)}, u32[]{:S(2)}) %collective-permute-start.22) | collective-permute-done | bytes 884768 | tf_op jit(solution)/shard_map/ppermute | solution.py:643
  149.0 1.7 %total.2 = bf16[192,2304]{1,0:T(8,128)(2,1)} custom-call(bf16[192,2304]{1,0:T(8,128)(2,1)S(1)} %copy-done.5, bf16[192,2304]{1,0:T(8,128)(2,1)S(1)} %collective-permute-done.18.refs_1_, bf16[192,2304]{1,0:T(8,128)(2,1)S(1)} %collective-permute-done.19.refs_2_, bf16[192,2304]{1,0:T(8,128)(2,1)S(1)} %collective-permute-done.20.refs_3_, bf16[384,384]{1,0:T(8,128)(2,1)S(1)} %copy-done), custom_call_target="tpu_custom_call" | custom-call | tf_op jit(solution)/shard_map/total/pallas_call | solution.py:621
  150.7 5.0 %collective-permute-done.27.refs_3_ = bf16[192,2304]{1,0:T(8,128)(2,1)S(1)} collective-permute-done((bf16[192,2304]{1,0:T(8,128)(2,1)S(1)}, bf16[192,2304]{1,0:T(8,128)(2,1)S(1)}, u32[]{:S(2)}, u32[]{:S(2)}) %collective-permute-start.27) | collective-permute-done | bytes 884768 | tf_op jit(solution)/shard_map/ppermute | solution.py:643
  155.8 6.1 %collective-permute-done.24.refs_2_ = bf16[192,2304]{1,0:T(8,128)(2,1)S(1)} collective-permute-done((bf16[192,2304]{1,0:T(8,128)(2,1)S(1)}, bf16[192,2304]{1,0:T(8,128)(2,1)S(1)}, u32[]{:S(2)}, u32[]{:S(2)}) %collective-permute-start.24) | collective-permute-done | bytes 884768 | tf_op jit(solution)/shard_map/ppermute | solution.py:643
  161.9 1.7 %total.3 = bf16[192,2304]{1,0:T(8,128)(2,1)} custom-call(bf16[192,2304]{1,0:T(8,128)(2,1)S(1)} %copy-done.6, bf16[192,2304]{1,0:T(8,128)(2,1)S(1)} %collective-permute-done.21.refs_1_, bf16[192,2304]{1,0:T(8,128)(2,1)S(1)} %collective-permute-done.24.refs_2_, bf16[192,2304]{1,0:T(8,128)(2,1)S(1)} %collective-permute-done.27.refs_3_, bf16[384,384]{1,0:T(8,128)(2,1)S(1)} %copy-done), custom_call_target="tpu_custom_call" | custom-call | tf_op jit(solution)/shard_map/total/pallas_call | solution.py:621
  (92 shorter events, 4.3 us)
Async XLA Ops:
  0.6 10.6 %copy-start.16 = (s32[4,1]{0,1:T(1,128)S(1)}, s32[4,1]{0,1:T(1,128)}, u32[]{:S(2)}) copy-start(s32[4,1]{0,1:T(1,128)} %param.16) | copy-start | bytes 52
  0.6 10.6 %copy-start.17 = (s32[4]{0:T(128)S(1)}, s32[4]{0:T(128)}, u32[]{:S(2)}) copy-start(s32[4]{0:T(128)} %param.15) | copy-start | bytes 52
  0.7 10.6 %copy-start.15 = (s32[4]{0:T(128)S(1)}, s32[4]{0:T(128)}, u32[]{:S(2)}) copy-start(s32[4]{0:T(128)} %param.17) | copy-start | bytes 52
  2.8 6.9 %copy-start.14 = (s32[512,3]{0,1:T(4,128)S(1)}, s32[512,3]{0,1:T(4,128)}, u32[]{:S(2)}) copy-start(s32[512,3]{0,1:T(4,128)} %param.18) | copy-start | bytes 18436
  2.8 11.4 %copy-start.2 = (bf16[384,384]{1,0:T(8,128)(2,1)S(1)}, bf16[384,384]{1,0:T(8,128)(2,1)}, u32[]{:S(2)}) copy-start(bf16[384,384]{1,0:T(8,128)(2,1)} %constant.33.clone.refs_2_.refs_1_) | copy-start | bytes 884740
  2.8 11.4 %copy-start.4 = (bf16[4,48,2304]{2,1,0:T(8,128)(2,1)S(1)}, bf16[4,48,2304]{2,1,0:T(8,128)(2,1)}, u32[]{:S(2)}) copy-start(bf16[4,48,2304]{2,1,0:T(8,128)(2,1)} %param.13) | copy-start | bytes 2654212
  3.5 20.8 %copy-start.8 = (bf16[192,2304]{1,0:T(8,128)(2,1)}, bf16[192,2304]{1,0:T(8,128)(2,1)S(1)}, u32[]{:S(2)}) copy-start(bf16[192,2304]{1,0:T(8,128)(2,1)S(1)} %reorder.3.refs_9_) | copy-start | bytes 2654212
  3.5 15.2 %collective-permute-start = (bf16[192,2304]{1,0:T(8,128)(2,1)S(1)}, bf16[192,2304]{1,0:T(8,128)(2,1)}, u32[]{:S(2)}, u32[]{:S(2)}) collective-permute-start(bf16[192,2304]{1,0:T(8,128)(2,1)S(1)} %reorder.3.refs_9_), channel_id=1, source_target_pairs={{0,1},{1,2},{2,3},{3,0},{4,5},{5,6},{6,7},{7,4},{8,9},{9,10},{10,1... | collective-permute-start | bytes 2654216 | tf_op jit(solution)/shard_map/ppermute | solution.py:643
  5.5 14.4 %collective-permute-start.1 = (bf16[192,2304]{1,0:T(8,128)(2,1)S(1)}, bf16[192,2304]{1,0:T(8,128)(2,1)}, u32[]{:S(2)}, u32[]{:S(2)}) collective-permute-start(bf16[192,2304]{1,0:T(8,128)(2,1)S(1)} %reorder.3.refs_9_), channel_id=1, source_target_pairs={{0,4},{1,5},{2,6},{3,7},{4,8},{5,9},{6,10},{7,11},{8,12},{9,13},{1... | collective-permute-start | bytes 2654216 | tf_op jit(solution)/shard_map/ppermute | solution.py:643
  7.0 13.3 %collective-permute-start.2 = (bf16[192,2304]{1,0:T(8,128)(2,1)S(1)}, bf16[192,2304]{1,0:T(8,128)(2,1)S(1)}, u32[]{:S(2)}, u32[]{:S(2)}) collective-permute-start(bf16[192,2304]{1,0:T(8,128)(2,1)S(1)} %reorder.3.refs_9_), channel_id=1, source_target_pairs={{0,112},{16,0},{32,16},{48,32},{64,48},{80,64},{96,80},{112,96},{1... | collective-permute-start | bytes 2654216 | tf_op jit(solution)/shard_map/ppermute | solution.py:651
  14.9 26.8 %copy-start.3 = (bf16[208,2304]{1,0:T(8,128)(2,1)}, bf16[208,2304]{1,0:T(8,128)(2,1)S(1)}, u32[]{:S(2)}) copy-start(bf16[208,2304]{1,0:T(8,128)(2,1)S(1)} %reorder.2.refs_1_) | copy-start | bytes 2875396
  20.3 16.6 %copy-start.21 = (bf16[192,2304]{1,0:T(8,128)(2,1)}, bf16[192,2304]{1,0:T(8,128)(2,1)S(1)}, u32[]{:S(2)}) copy-start(bf16[192,2304]{1,0:T(8,128)(2,1)S(1)} %collective-permute-done.2.refs_16_) | copy-start | bytes 2654212
  20.3 15.0 %collective-permute-start.3 = (bf16[208,2304]{1,0:T(8,128)(2,1)S(1)}, bf16[208,2304]{1,0:T(8,128)(2,1)S(1)}, u32[]{:S(2)}, u32[]{:S(2)}) collective-permute-start(bf16[208,2304]{1,0:T(8,128)(2,1)S(1)} %reorder.2.refs_1_), channel_id=1, source_target_pairs={{0,1},{1,2},{2,3},{3,0},{4,5},{5,6},{6,7},{7,4},{8,9},{9,10},{10,1... | collective-permute-start | bytes 2875400 | tf_op jit(solution)/shard_map/ppermute | solution.py:643
  21.8 15.0 %collective-permute-start.4 = (bf16[208,2304]{1,0:T(8,128)(2,1)S(1)}, bf16[208,2304]{1,0:T(8,128)(2,1)S(1)}, u32[]{:S(2)}, u32[]{:S(2)}) collective-permute-start(bf16[208,2304]{1,0:T(8,128)(2,1)S(1)} %reorder.2.refs_1_), channel_id=1, source_target_pairs={{0,4},{1,5},{2,6},{3,7},{4,8},{5,9},{6,10},{7,11},{8,12},{9,13},{1... | collective-permute-start | bytes 2875400 | tf_op jit(solution)/shard_map/ppermute | solution.py:643
  22.1 14.8 %collective-permute-start.5 = (bf16[208,2304]{1,0:T(8,128)(2,1)S(1)}, bf16[208,2304]{1,0:T(8,128)(2,1)S(1)}, u32[]{:S(2)}, u32[]{:S(2)}) collective-permute-start(bf16[208,2304]{1,0:T(8,128)(2,1)S(1)} %reorder.2.refs_1_), channel_id=1, source_target_pairs={{0,112},{16,0},{32,16},{48,32},{64,48},{80,64},{96,80},{112,96},{1... | collective-permute-start | bytes 2875400 | tf_op jit(solution)/shard_map/ppermute | solution.py:651
  35.3 21.0 %copy-start.13 = (bf16[208,2304]{1,0:T(8,128)(2,1)}, bf16[208,2304]{1,0:T(8,128)(2,1)S(1)}, u32[]{:S(2)}) copy-start(bf16[208,2304]{1,0:T(8,128)(2,1)S(1)} %collective-permute-done.3.refs_2_) | copy-start | bytes 2875396
  36.9 17.9 %copy-start.12 = (bf16[208,2304]{1,0:T(8,128)(2,1)}, bf16[208,2304]{1,0:T(8,128)(2,1)S(1)}, u32[]{:S(2)}) copy-start(bf16[208,2304]{1,0:T(8,128)(2,1)S(1)} %collective-permute-done.4.refs_3_) | copy-start | bytes 2875396
  36.9 19.4 %collective-permute-start.8 = (bf16[208,2304]{1,0:T(8,128)(2,1)S(1)}, bf16[208,2304]{1,0:T(8,128)(2,1)S(1)}, u32[]{:S(2)}, u32[]{:S(2)}) collective-permute-start(bf16[208,2304]{1,0:T(8,128)(2,1)S(1)} %collective-permute-done.4.refs_3_), channel_id=1, source_target_pairs={{0,3},{1,0},{2,1},{3,2},{4,7},{5,4},{6,5},{7,6},{8,11},{9,8},{10,9... | collective-permute-start | bytes 2875400 | tf_op jit(solution)/shard_map/ppermute | solution.py:643
  38.7 18.6 %collective-permute-start.9 = (bf16[208,2304]{1,0:T(8,128)(2,1)S(1)}, bf16[208,2304]{1,0:T(8,128)(2,1)S(1)}, u32[]{:S(2)}, u32[]{:S(2)}) collective-permute-start(bf16[208,2304]{1,0:T(8,128)(2,1)S(1)} %collective-permute-done.3.refs_2_), channel_id=1, source_target_pairs={{0,12},{1,13},{2,14},{3,15},{4,0},{5,1},{6,2},{7,3},{8,4},{9,5},{1... | collective-permute-start | bytes 2875400 | tf_op jit(solution)/shard_map/ppermute | solution.py:643
  38.8 16.0 %collective-permute-start.7 = (bf16[112,2304]{1,0:T(8,128)(2,1)S(1)}, bf16[112,2304]{1,0:T(8,128)(2,1)S(1)}, u32[]{:S(2)}, u32[]{:S(2)}) collective-permute-start(bf16[112,2304]{1,0:T(8,128)(2,1)S(1)} %slice.36), channel_id=1, source_target_pairs={{0,1},{1,2},{2,3},{3,0},{4,5},{5,6},{6,7},{7,4},{8,9},{9,10},{10,1... | collective-permute-start | bytes 1548296 | tf_op jit(solution)/shard_map/ppermute | solution.py:643
  40.0 14.4 %collective-permute-start.6 = (bf16[96,2304]{1,0:T(8,128)(2,1)S(1)}, bf16[96,2304]{1,0:T(8,128)(2,1)S(1)}, u32[]{:S(2)}, u32[]{:S(2)}) collective-permute-start(bf16[96,2304]{1,0:T(8,128)(2,1)S(1)} %slice.35), channel_id=1, source_target_pairs={{0,4},{1,5},{2,6},{3,7},{4,8},{5,9},{6,10},{7,11},{8,12},{9,13},{1... | collective-permute-start | bytes 1327112 | tf_op jit(solution)/shard_map/ppermute | solution.py:643
  54.8 7.4 %copy-start.24 = (bf16[112,2304]{1,0:T(8,128)(2,1)}, bf16[112,2304]{1,0:T(8,128)(2,1)S(1)}, u32[]{:S(2)}) copy-start(bf16[112,2304]{1,0:T(8,128)(2,1)S(1)} %collective-permute-done.7.refs_5_) | copy-start | bytes 1548292
  56.3 5.8 %copy-start.18 = (bf16[208,2304]{1,0:T(8,128)(2,1)}, bf16[208,2304]{1,0:T(8,128)(2,1)S(1)}, u32[]{:S(2)}) copy-start(bf16[208,2304]{1,0:T(8,128)(2,1)S(1)} %collective-permute-done.8.refs_6_) | copy-start | bytes 2875396
  57.2 4.9 %copy-start.19 = (bf16[208,2304]{1,0:T(8,128)(2,1)}, bf16[208,2304]{1,0:T(8,128)(2,1)S(1)}, u32[]{:S(2)}) copy-start(bf16[208,2304]{1,0:T(8,128)(2,1)S(1)} %collective-permute-done.9.refs_7_) | copy-start | bytes 2875396
  58.1 20.3 %collective-permute-start.12 = (bf16[192,2304]{1,0:T(8,128)(2,1)}, bf16[192,2304]{1,0:T(8,128)(2,1)S(1)}, u32[]{:S(2)}, u32[]{:S(2)}) collective-permute-start(bf16[192,2304]{1,0:T(8,128)(2,1)} %collective-permute-done.1.refs_11_), channel_id=1, source_target_pairs={{0,3},{1,0},{2,1},{3,2},{4,7},{5,4},{6,5},{7,6},{8,11},{9,8},{10,9... | collective-permute-start | bytes 2654216 | tf_op jit(solution)/shard_map/ppermute | solution.py:643
  60.1 25.7 %collective-permute-start.13 = (bf16[192,2304]{1,0:T(8,128)(2,1)}, bf16[192,2304]{1,0:T(8,128)(2,1)S(1)}, u32[]{:S(2)}, u32[]{:S(2)}) collective-permute-start(bf16[192,2304]{1,0:T(8,128)(2,1)} %collective-permute-done.refs_10_), channel_id=1, source_target_pairs={{0,12},{1,13},{2,14},{3,15},{4,0},{5,1},{6,2},{7,3},{8,4},{9,5},{1... | collective-permute-start | bytes 2654216 | tf_op jit(solution)/shard_map/ppermute | solution.py:643
  60.4 14.6 %collective-permute-start.10 = (bf16[96,2304]{1,0:T(8,128)(2,1)S(1)}, bf16[96,2304]{1,0:T(8,128)(2,1)S(1)}, u32[]{:S(2)}, u32[]{:S(2)}) collective-permute-start(bf16[96,2304]{1,0:T(8,128)(2,1)S(1)} %slice.31), channel_id=1, source_target_pairs={{0,4},{1,5},{2,6},{3,7},{4,8},{5,9},{6,10},{7,11},{8,12},{9,13},{1... | collective-permute-start | bytes 1327112 | tf_op jit(solution)/shard_map/ppermute | solution.py:643
  62.1 15.5 %collective-permute-start.11 = (bf16[96,2304]{1,0:T(8,128)(2,1)S(1)}, bf16[96,2304]{1,0:T(8,128)(2,1)S(1)}, u32[]{:S(2)}, u32[]{:S(2)}) collective-permute-start(bf16[96,2304]{1,0:T(8,128)(2,1)S(1)} %slice.32), channel_id=1, source_target_pairs={{0,1},{1,2},{2,3},{3,0},{4,5},{5,6},{6,7},{7,4},{8,9},{9,10},{10,1... | collective-permute-start | bytes 1327112 | tf_op jit(solution)/shard_map/ppermute | solution.py:643
  74.9 26.5 %collective-permute-start.14 = (bf16[192,2304]{1,0:T(8,128)(2,1)}, bf16[192,2304]{1,0:T(8,128)(2,1)S(1)}, u32[]{:S(2)}, u32[]{:S(2)}) collective-permute-start(bf16[192,2304]{1,0:T(8,128)(2,1)} %get-tuple-element.94), channel_id=1, source_target_pairs={{0,1},{1,2},{2,3},{3,0},{4,5},{5,6},{6,7},{7,4},{8,9},{9,10},{10,1... | collective-permute-start | bytes 2654216 | tf_op jit(solution)/shard_map/ppermute | solution.py:643
  75.0 26.4 %collective-permute-start.15 = (bf16[192,2304]{1,0:T(8,128)(2,1)}, bf16[192,2304]{1,0:T(8,128)(2,1)S(1)}, u32[]{:S(2)}, u32[]{:S(2)}) collective-permute-start(bf16[192,2304]{1,0:T(8,128)(2,1)} %get-tuple-element.95), channel_id=1, source_target_pairs={{0,4},{1,5},{2,6},{3,7},{4,8},{5,9},{6,10},{7,11},{8,12},{9,13},{1... | collective-permute-start | bytes 2654216 | tf_op jit(solution)/shard_map/ppermute | solution.py:643
  78.4 23.0 %collective-permute-start.18 = (bf16[192,2304]{1,0:T(8,128)(2,1)}, bf16[192,2304]{1,0:T(8,128)(2,1)S(1)}, u32[]{:S(2)}, u32[]{:S(2)}) collective-permute-start(bf16[192,2304]{1,0:T(8,128)(2,1)} %get-tuple-element.96), channel_id=1, source_target_pairs={{0,16},{16,32},{32,48},{48,64},{64,80},{80,96},{96,112},{112,0},{1... | collective-permute-start | bytes 2654216 | tf_op jit(solution)/shard_map/ppermute | solution.py:651
  79.3 22.0 %collective-permute-start.16 = (bf16[96,2304]{1,0:T(8,128)(2,1)}, bf16[96,2304]{1,0:T(8,128)(2,1)S(1)}, u32[]{:S(2)}, u32[]{:S(2)}) collective-permute-start(bf16[96,2304]{1,0:T(8,128)(2,1)} %get-tuple-element.92), channel_id=1, source_target_pairs={{0,12},{1,13},{2,14},{3,15},{4,0},{5,1},{6,2},{7,3},{8,4},{9,5},{1... | collective-permute-start | bytes 1327112 | tf_op jit(solution)/shard_map/ppermute | solution.py:643
  85.8 15.6 %collective-permute-start.17 = (bf16[96,2304]{1,0:T(8,128)(2,1)}, bf16[96,2304]{1,0:T(8,128)(2,1)S(1)}, u32[]{:S(2)}, u32[]{:S(2)}) collective-permute-start(bf16[96,2304]{1,0:T(8,128)(2,1)} %get-tuple-element.93), channel_id=1, source_target_pairs={{0,3},{1,0},{2,1},{3,2},{4,7},{5,4},{6,5},{7,6},{8,11},{9,8},{10,9... | collective-permute-start | bytes 1327112 | tf_op jit(solution)/shard_map/ppermute | solution.py:643
  89.0 12.4 %copy-start.11 = (bf16[192,2304]{1,0:T(8,128)(2,1)S(1)}, bf16[192,2304]{1,0:T(8,128)(2,1)}, u32[]{:S(2)}) copy-start(bf16[192,2304]{1,0:T(8,128)(2,1)} %get-tuple-element.139) | copy-start | bytes 2654212
  101.4 7.6 %copy-start.10 = (bf16[192,2304]{1,0:T(8,128)(2,1)S(1)}, bf16[192,2304]{1,0:T(8,128)(2,1)}, u32[]{:S(2)}) copy-start(bf16[192,2304]{1,0:T(8,128)(2,1)} %get-tuple-element.136) | copy-start | bytes 2654212
  101.7 20.4 %collective-permute-start.20 = (bf16[192,2304]{1,0:T(8,128)(2,1)S(1)}, bf16[192,2304]{1,0:T(8,128)(2,1)S(1)}, u32[]{:S(2)}, u32[]{:S(2)}) collective-permute-start(bf16[192,2304]{1,0:T(8,128)(2,1)S(1)} %add_convert_fusion.2), channel_id=1, source_target_pairs={{0,12},{1,13},{2,14},{3,15},{4,0},{5,1},{6,2},{7,3},{8,4},{9,5},{1... | collective-permute-start | bytes 2654216 | tf_op jit(solution)/shard_map/ppermute | solution.py:643
  109.3 16.9 %collective-permute-start.19 = (bf16[192,2304]{1,0:T(8,128)(2,1)S(1)}, bf16[192,2304]{1,0:T(8,128)(2,1)S(1)}, u32[]{:S(2)}, u32[]{:S(2)}) collective-permute-start(bf16[192,2304]{1,0:T(8,128)(2,1)S(1)} %add_convert_fusion.3), channel_id=1, source_target_pairs={{0,3},{1,0},{2,1},{3,2},{4,7},{5,4},{6,5},{7,6},{8,11},{9,8},{10,9... | collective-permute-start | bytes 2654216 | tf_op jit(solution)/shard_map/ppermute | solution.py:643
  122.1 26.4 %copy-start.9 = (bf16[192,2304]{1,0:T(8,128)(2,1)S(1)}, bf16[192,2304]{1,0:T(8,128)(2,1)}, u32[]{:S(2)}) copy-start(bf16[192,2304]{1,0:T(8,128)(2,1)} %get-tuple-element.146) | copy-start | bytes 2654212
  126.2 14.5 %collective-permute-start.25 = (bf16[192,2304]{1,0:T(8,128)(2,1)}, bf16[192,2304]{1,0:T(8,128)(2,1)S(1)}, u32[]{:S(2)}, u32[]{:S(2)}) collective-permute-start(bf16[192,2304]{1,0:T(8,128)(2,1)} %get-tuple-element.150), channel_id=1, source_target_pairs={{0,1},{1,2},{2,3},{3,0},{4,5},{5,6},{6,7},{7,4},{8,9},{9,10},{10,1... | collective-permute-start | bytes 2654216 | tf_op jit(solution)/shard_map/ppermute | solution.py:643
  126.2 10.4 %collective-permute-start.26 = (bf16[96,2304]{1,0:T(8,128)(2,1)}, bf16[96,2304]{1,0:T(8,128)(2,1)S(1)}, u32[]{:S(2)}, u32[]{:S(2)}) collective-permute-start(bf16[96,2304]{1,0:T(8,128)(2,1)} %get-tuple-element.151), channel_id=1, source_target_pairs={{0,3},{1,0},{2,1},{3,2},{4,7},{5,4},{6,5},{7,6},{8,11},{9,8},{10,9... | collective-permute-start | bytes 1327112 | tf_op jit(solution)/shard_map/ppermute | solution.py:643
  129.4 19.1 %collective-permute-start.22 = (bf16[192,2304]{1,0:T(8,128)(2,1)}, bf16[192,2304]{1,0:T(8,128)(2,1)S(1)}, u32[]{:S(2)}, u32[]{:S(2)}) collective-permute-start(bf16[192,2304]{1,0:T(8,128)(2,1)} %get-tuple-element.147), channel_id=1, source_target_pairs={{0,4},{1,5},{2,6},{3,7},{4,8},{5,9},{6,10},{7,11},{8,12},{9,13},{1... | collective-permute-start | bytes 2654216 | tf_op jit(solution)/shard_map/ppermute | solution.py:643
  129.4 15.3 %collective-permute-start.23 = (bf16[96,2304]{1,0:T(8,128)(2,1)}, bf16[96,2304]{1,0:T(8,128)(2,1)S(1)}, u32[]{:S(2)}, u32[]{:S(2)}) collective-permute-start(bf16[96,2304]{1,0:T(8,128)(2,1)} %get-tuple-element.148), channel_id=1, source_target_pairs={{0,12},{1,13},{2,14},{3,15},{4,0},{5,1},{6,2},{7,3},{8,4},{9,5},{1... | collective-permute-start | bytes 1327112 | tf_op jit(solution)/shard_map/ppermute | solution.py:643
  132.7 18.1 %collective-permute-start.21 = (bf16[192,2304]{1,0:T(8,128)(2,1)}, bf16[192,2304]{1,0:T(8,128)(2,1)S(1)}, u32[]{:S(2)}, u32[]{:S(2)}) collective-permute-start(bf16[192,2304]{1,0:T(8,128)(2,1)} %get-tuple-element.145), channel_id=1, source_target_pairs={{0,16},{16,32},{32,48},{48,64},{64,80},{80,96},{96,112},{112,0},{1... | collective-permute-start | bytes 2654216 | tf_op jit(solution)/shard_map/ppermute | solution.py:651
  142.1 6.9 %copy-start = (bf16[384,384]{1,0:T(8,128)(2,1)S(1)}, bf16[384,384]{1,0:T(8,128)(2,1)}, u32[]{:S(2)}) copy-start(bf16[384,384]{1,0:T(8,128)(2,1)} %constant.34.clone.refs_4_) | copy-start | bytes 884740
  142.1 6.9 %copy-start.5 = (bf16[192,2304]{1,0:T(8,128)(2,1)S(1)}, bf16[192,2304]{1,0:T(8,128)(2,1)}, u32[]{:S(2)}) copy-start(bf16[192,2304]{1,0:T(8,128)(2,1)} %get-tuple-element.118.refs_0_) | copy-start | bytes 2654212
  142.1 13.7 %collective-permute-start.27 = (bf16[192,2304]{1,0:T(8,128)(2,1)S(1)}, bf16[192,2304]{1,0:T(8,128)(2,1)S(1)}, u32[]{:S(2)}, u32[]{:S(2)}) collective-permute-start(bf16[192,2304]{1,0:T(8,128)(2,1)S(1)} %add_convert_fusion), channel_id=1, source_target_pairs={{0,12},{1,13},{2,14},{3,15},{4,0},{5,1},{6,2},{7,3},{8,4},{9,5},{1... | collective-permute-start | bytes 2654216 | tf_op jit(solution)/shard_map/ppermute | solution.py:643
  148.8 13.1 %copy-start.6 = (bf16[192,2304]{1,0:T(8,128)(2,1)S(1)}, bf16[192,2304]{1,0:T(8,128)(2,1)}, u32[]{:S(2)}) copy-start(bf16[192,2304]{1,0:T(8,128)(2,1)} %get-tuple-element.144.refs_0_) | copy-start | bytes 2654212
  148.8 13.1 %collective-permute-start.24 = (bf16[192,2304]{1,0:T(8,128)(2,1)S(1)}, bf16[192,2304]{1,0:T(8,128)(2,1)S(1)}, u32[]{:S(2)}, u32[]{:S(2)}) collective-permute-start(bf16[192,2304]{1,0:T(8,128)(2,1)S(1)} %add_convert_fusion.1), channel_id=1, source_target_pairs={{0,3},{1,0},{2,1},{3,2},{4,7},{5,4},{6,5},{7,6},{8,11},{9,8},{10,9... | collective-permute-start | bytes 2654216 | tf_op jit(solution)/shard_map/ppermute | solution.py:643
  (8 other events, 14.4 us)
where the time goes:
time: 165 us; the launch traced here: 164 us
  waiting for transfers between devices  59.5 us (36%)
  starting transfers between devices  47 us (28%)
  Pallas kernels  44.3 us (27%)
  local copies, waits for them, and re-layouts  7.18 us (4%)
  other arithmetic  4.72 us (3%)
    ppermute x24, waiting for transfers between devices, move(): return lax.ppermute(block, ('region', 'sub'), pairs)  59.1 us
    ppermute x24, starting transfers between devices, move(): return lax.ppermute(block, ('region', 'sub'), pairs)  43.1 us
    pallas_call x3, Pallas kernels, exchange(): pl.pallas_call(kernel, out_shape=outs, in_specs=[smem] + [any_space] * (l...  37.8 us
    unnamed x57, local copies, waits for them, and re-layouts  4.09 us
    ppermute x4, starting transfers between devices, move(): return lax.ppermute(block, 'region', pairs)  3.88 us
    pallas_call x2, Pallas kernels, total(): pl.pallas_call(total_kernel, grid=(2,), out_shape=jax.ShapeDtypeStruct((S...  3.43 us
  transfers between devices with their start and end apart: 28, of which 15 were waited for; matrix products, arithmetic and copies ran while one was open for 4% of the time, Pallas kernels for 26%

commit v1 on v0

--- a/solution.py
+++ b/solution.py
@@ -27,8 +27,8 @@
 LISTED = PAIRS_DEV * LIST_WIDTH
 NOTE_ROWS = 16
 SET_ROWS = ORB_DEV * BOX
-SIZES = (4, 4, 4, 2, 2, 4, 4, 4)
-N_OUT = len(SIZES)
+GIVEN = (tuple(range(SOURCES)), tuple(range(SOURCES)), (0, 1, 2, REGION_SOURCE))
+FAR_PLACES = (3, 4, 5)
 N_TABLES = 4
 BLOCKS_Y = 6
 BLOCKS_Z = 3
@@ -330,13 +330,14 @@
 def exchange_kernel(part, *refs):
     second = part > 0
     sets = 2 if second else 1
-    carried = N_OUT if part == 2 else 0
+    given = GIVEN[part]
+    carried = len(given) if part == 2 else 0
     n_in = sets * (SOURCES + 1)
     listing, *refs = refs
     boxes_in, refs = refs[:n_in], refs[n_in:]
     tables_in, refs = refs[:N_TABLES], refs[N_TABLES:]
     sums_in, refs = refs[:carried], refs[carried:]
-    outs, refs = refs[:N_OUT], refs[N_OUT:]
+    outs, refs = refs[: len(given)], refs[len(given) :]
     tables, refs = refs[:N_TABLES], refs[N_TABLES:]
     acc, stage, held, theirs, both, work, padded, mine, sems, table_sems, out_sems = refs
 
@@ -346,8 +347,15 @@
         def check(pair, carry, home=home):
             row = (home * PAIRS_DEV + pair) * LIST_WIDTH
             for kind in (1, 2) if second else (0,):
-
-                @pl.when(listing[row + 2 * kind] == home)
+                here = listing[row + 2 * kind] == home
+                if second:
+                    gives_far = jnp.bool_(home in FAR_PLACES)
+                    if kind == 2:
+                        source = listing[row + 2 * kind + 1]
+                        gives_far = (source >= FAR_PLACES[0]) & (source <= FAR_PLACES[-1])
+                    here &= gives_far if part == 1 else jnp.logical_not(gives_far)
+
+                @pl.when(here)
                 def _(kind=kind):
                     at = mine[0]
                     mine[0] = at + 1
@@ -364,9 +372,7 @@
 
     count = mine[0]
     steps = (count + 1) >> 1
-    half = (steps + 1) >> 1
-    begin = half if part == 2 else 0
-    end = half if part == 1 else steps
+    begin, end = 0, steps
 
     def table_copies():
         return [
@@ -431,9 +437,8 @@
 
     def sum_copies(into):
         copies = []
-        for i, size in enumerate(SIZES):
-            low = sum(SIZES[:i]) * BOX
-            vmem = stage.at[pl.ds(low, size * BOX)]
+        for i, source in enumerate(given):
+            vmem = stage.at[pl.ds(source * SET_ROWS, SET_ROWS)]
             if into:
                 copies.append(pltpu.make_async_copy(sums_in[i], vmem, out_sems.at[i]))
             else:
@@ -460,7 +465,9 @@
 
     def prepare(i, carry):
         if carried:
-            acc[box_rows(i), :] = stage[box_rows(i), :].astype(F32)
+            keep = stage[box_rows(i), :].astype(F32)
+            is_given = (i < 3 * ORB_DEV) | (i >= REGION_SOURCE * ORB_DEV)
+            acc[box_rows(i), :] = jnp.where(is_given, keep, 0.0)
         else:
             acc[box_rows(i), :] = jnp.zeros((BOX, PLANE), F32)
         return carry
@@ -528,16 +535,14 @@
     lax.fori_loop(begin, end, one_step, 0)
 
     copies = sum_copies(False)
-    at = 0
-    for copy, size in zip(copies, SIZES):
+    for copy, source in zip(copies, given):
 
         def put(i, carry):
             stage[box_rows(i), :] = acc[box_rows(i), :].astype(BF16)
             return carry
 
-        lax.fori_loop(at, at + size, put, 0)
+        lax.fori_loop(source * ORB_DEV, (source + 1) * ORB_DEV, put, 0)
         copy.start()
-        at += size
     for copy in copies:
         copy.wait()
 
@@ -546,7 +551,7 @@
     any_space = pl.BlockSpec(memory_space=pl.ANY)
     smem = pl.BlockSpec(memory_space=pltpu.SMEM)
     outs = [
-        jax.ShapeDtypeStruct((size * BOX, PLANE), BF16) for size in SIZES
+        jax.ShapeDtypeStruct((SET_ROWS, PLANE), BF16) for _ in GIVEN[part]
     ]
 
     def kernel(*refs):
@@ -569,7 +574,7 @@
             pltpu.SMEM(((MAX_TASKS + 3) * TASK_WIDTH,), jnp.int32),
             pltpu.SemaphoreType.DMA((2, 4)),
             pltpu.SemaphoreType.DMA((N_TABLES,)),
-            pltpu.SemaphoreType.DMA((N_OUT,)),
+            pltpu.SemaphoreType.DMA((SOURCES,)),
         ],
         compiler_params=pltpu.CompilerParams(vmem_limit_bytes=56 * 1024 * 1024),
         cost_estimate=pl.CostEstimate(
@@ -694,26 +699,16 @@
         return step(1, 0)(low), step(0, 1)(high), step(0, -1)(b10), step(-1, 0)(b01)
 
     def begin_back(parts):
-        own, c01, c10, c11_low, c11_high, c13, c31, c_abroad = parts
-        return (
-            step(0, 1)(c13),
-            step(1, 0)(c31),
-            step(-1, 0)(c11_low),
-            step(0, -1)(c11_high),
-            across(1)(c_abroad),
-        )
-
-    def merge(parts, arrived):
-        r13, r31, r11_low, r11_high, _ = arrived
-        none = jnp.zeros_like(r11_low)
-        low = jnp.concatenate([r11_low, none])
-        high = jnp.concatenate([none, r11_high])
-        m01 = (parts[1].astype(F32) + r31.astype(F32) + low.astype(F32)).astype(BF16)
-        m10 = (parts[2].astype(F32) + r13.astype(F32) + high.astype(F32)).astype(BF16)
+        return step(-1, 0)(parts[3]), step(0, 1)(parts[4]), step(1, 0)(parts[5])
+
+    def merge(c01, c10, arrived):
+        r11, r13, r31 = arrived
+        m01 = (c01.astype(F32) + r31.astype(F32) + r11.astype(F32)).astype(BF16)
+        m10 = (c10.astype(F32) + r13.astype(F32)).astype(BF16)
         return step(0, -1)(m01), step(-1, 0)(m10)
 
-    def finish(parts, arrived, merged):
-        result = total([parts[0], arrived[4], *merged], order_back)
+    def finish(own, abroad, merged):
+        result = total([own, abroad, *merged], order_back)
         return result.reshape(ORB_DEV, BOX, PLANE)
 
     ordered = lax.optimization_barrier
@@ -733,17 +728,20 @@
     listing = jnp.concatenate([n[-NOTE_ROWS, :LISTED] for n in notes]).astype(jnp.int32)
     first = exchange(0, listing, orbital_boxes, tables)
     arrived_first = begin_back(first)
+    abroad_first = across(1)(first[6])
     first, listing, t_far = ordered((first, listing, t_far))
     all_boxes = orbital_boxes + [trials, t01, t10, *t_far, t_abroad]
     early = exchange(1, listing, all_boxes, tables)
-    early, first, arrived_first = ordered((early, first, arrived_first))
-    merged_first = merge(first, arrived_first)
-    late = exchange(2, listing, all_boxes, tables, early)
-    late, merged_first = ordered((late, merged_first))
-    result_first = finish(first, arrived_first, merged_first)
-    arrived_late = begin_back(late)
-    result_second = finish(late, arrived_late, merge(late, arrived_late))
-    return result_first, result_second
+    early, first, arrived_first, abroad_first = ordered((early, first, arrived_first, abroad_first))
+    merged_first = merge(first[1], first[2], arrived_first)
+    arrived_second = begin_back(early)
+    late = exchange(2, listing, all_boxes, tables, [early[i] for i in GIVEN[2]])
+    late, merged_first, arrived_second = ordered((late, merged_first, arrived_second))
+    own, c01, c10, c_abroad = late
+    abroad_second = across(1)(c_abroad)
+    merged_second = merge(c01, c10, arrived_second)
+    result_first = finish(first[0], abroad_first, merged_first)
+    return result_first, finish(own, abroad_second, merged_second)
 
 
 def solution(mesh):

time: 165 us -> 157 us (0.952)
  the two profiles are of different devices: /device:TPU:8 before, /device:TPU:0 now
where the time goes in v1:
time: 157 us
  waiting for transfers between devices  53.5 us (34%)
  Pallas kernels  50.1 us (32%)
  starting transfers between devices  38.4 us (24%)
  local copies, waits for them, and re-layouts  8.83 us (6%)
  other arithmetic  4.79 us (3%)
    ppermute x22, waiting for transfers between devices, move(): return lax.ppermute(block, ('region', 'sub'), pairs)  49.8 us
    pallas_call x3, Pallas kernels, exchange(): pl.pallas_call(kernel, out_shape=outs, in_specs=[smem] + [any_space] * (l...  43.5 us
    ppermute x22, starting transfers between devices, move(): return lax.ppermute(block, ('region', 'sub'), pairs)  29.3 us
    ppermute x4, starting transfers between devices, move(): return lax.ppermute(block, 'region', pairs)  9.08 us
    unnamed x61, local copies, waits for them, and re-layouts  5.75 us
    ppermute x4, waiting for transfers between devices, move(): return lax.ppermute(block, 'region', pairs)  3.73 us
    pallas_call x2, Pallas kernels, total(): pl.pallas_call(total_kernel, grid=(2,), out_shape=jax.ShapeDtypeStruct((S...  3.45 us
  transfers between devices with their start and end apart: 26, of which 15 were waited for; matrix products, arithmetic and copies ran while one was open for 4% of the time, Pallas kernels for 30%

profile of v1, /device:TPU:0, one launch (start us, length us, event | category | flops | bytes accessed | tf_op | source)
XLA Modules:
  0.0 156.6 jit_solution(16466144811754195513)
XLA Ops:
  0.7 1.0 copy-done.1
  1.6 1.2 copy-done.7
  2.8 0.7 reorder.3.refs_9_
  3.5 2.1 %collective-permute-start = (bf16[192,2304]{1,0:T(8,128)(2,1)S(1)}, bf16[192,2304]{1,0:T(8,128)(2,1)}, u32[]{:S(2)}, u32[]{:S(2)}) collective-permute-start(bf16[192,2304]{1,0:T(8,128)(2,1)S(1)} %reorder.3.refs_9_), channel_id=1, source_target_pairs={{0,1},{1,2},{2,3},{3,0},{4,5},{5,6},{6,7},{7,4},{8,9},{9,10},{10,1... | collective-permute-start | bytes 2654216 | tf_op jit(solution)/shard_map/ppermute | solution.py:648
  5.6 1.5 collective-permute-start.1
  7.1 5.3 %collective-permute-start.2 = (bf16[192,2304]{1,0:T(8,128)(2,1)S(1)}, bf16[192,2304]{1,0:T(8,128)(2,1)S(1)}, u32[]{:S(2)}, u32[]{:S(2)}) collective-permute-start(bf16[192,2304]{1,0:T(8,128)(2,1)S(1)} %reorder.3.refs_9_), channel_id=1, source_target_pairs={{0,112},{16,0},{32,16},{48,32},{64,48},{80,64},{96,80},{112,96},{1... | collective-permute-start | bytes 2654216 | tf_op jit(solution)/shard_map/ppermute | solution.py:656
  12.5 0.8 reshape.20.refs_2_
  13.9 0.6 pad_add_fusion.1.refs_1_
  14.5 1.7 %plan.1 = s32[64]{0:T(128)} custom-call(s32[3]{0:T(128)} %pad_add_fusion.refs_0_, s32[12]{0:T(128)} %pad_add_fusion.1.refs_1_, s32[1536]{0:T(1024)} %reshape.20.refs_2_, s32[112]{0:T(128)} %constant.34.clone.refs_3_), custom_call_target="tpu_custom_call" | custom-call | tf_op jit(solution)/shard_map/plan/pallas_call | solution.py:682
  16.2 0.6 convert_bitcast_fusion
  16.8 0.7 reorder.2.refs_1_
  17.6 1.3 collective-permute-done.refs_10_
  18.9 1.1 collective-permute-done.1.refs_11_
  20.0 3.0 %collective-permute-done.2.refs_16_ = bf16[192,2304]{1,0:T(8,128)(2,1)S(1)} collective-permute-done((bf16[192,2304]{1,0:T(8,128)(2,1)S(1)}, bf16[192,2304]{1,0:T(8,128)(2,1)S(1)}, u32[]{:S(2)}, u32[]{:S(2)}) %collective-permute-start.2) | collective-permute-done | bytes 884768 | tf_op jit(solution)/shard_map/ppermute | solution.py:656
  23.0 3.8 %collective-permute-start.5 = (bf16[208,2304]{1,0:T(8,128)(2,1)S(1)}, bf16[208,2304]{1,0:T(8,128)(2,1)S(1)}, u32[]{:S(2)}, u32[]{:S(2)}) collective-permute-start(bf16[208,2304]{1,0:T(8,128)(2,1)S(1)} %reorder.2.refs_1_), channel_id=1, source_target_pairs={{0,112},{16,0},{32,16},{48,32},{64,48},{80,64},{96,80},{112,96},{1... | collective-permute-start | bytes 2875400 | tf_op jit(solution)/shard_map/ppermute | solution.py:656
  26.7 1.0 slice.31
  27.8 1.0 slice.32
  28.8 9.2 %collective-permute-done.3.refs_2_ = bf16[208,2304]{1,0:T(8,128)(2,1)S(1)} collective-permute-done((bf16[208,2304]{1,0:T(8,128)(2,1)S(1)}, bf16[208,2304]{1,0:T(8,128)(2,1)S(1)}, u32[]{:S(2)}, u32[]{:S(2)}) %collective-permute-start.3) | collective-permute-done | bytes 958496 | tf_op jit(solution)/shard_map/ppermute | solution.py:648
  38.1 3.2 %collective-permute-start.8 = (bf16[208,2304]{1,0:T(8,128)(2,1)S(1)}, bf16[208,2304]{1,0:T(8,128)(2,1)S(1)}, u32[]{:S(2)}, u32[]{:S(2)}) collective-permute-start(bf16[208,2304]{1,0:T(8,128)(2,1)S(1)} %collective-permute-done.4.refs_3_), channel_id=1, source_target_pairs={{0,3},{1,0},{2,1},{3,2},{4,7},{5,4},{6,5},{7,6},{8,11},{9,8},{10,9... | collective-permute-start | bytes 2875400 | tf_op jit(solution)/shard_map/ppermute | solution.py:648
  41.5 2.1 %collective-permute-start.6 = (bf16[96,2304]{1,0:T(8,128)(2,1)S(1)}, bf16[96,2304]{1,0:T(8,128)(2,1)S(1)}, u32[]{:S(2)}, u32[]{:S(2)}) collective-permute-start(bf16[96,2304]{1,0:T(8,128)(2,1)S(1)} %slice.35), channel_id=1, source_target_pairs={{0,4},{1,5},{2,6},{3,7},{4,8},{5,9},{6,10},{7,11},{8,12},{9,13},{1... | collective-permute-start | bytes 1327112 | tf_op jit(solution)/shard_map/ppermute | solution.py:648
  43.6 12.3 %collective-permute-done.6.refs_4_ = bf16[96,2304]{1,0:T(8,128)(2,1)S(1)} collective-permute-done((bf16[96,2304]{1,0:T(8,128)(2,1)S(1)}, bf16[96,2304]{1,0:T(8,128)(2,1)S(1)}, u32[]{:S(2)}, u32[]{:S(2)}) %collective-permute-start.6) | collective-permute-done | bytes 442400 | tf_op jit(solution)/shard_map/ppermute | solution.py:648
  55.9 0.6 collective-permute-done.7.refs_5_
  56.9 0.7 collective-permute-done.9.refs_7_
  57.7 0.7 convert_element_type.51.refs_0_
  58.4 2.2 %collective-permute-start.12 = (bf16[192,2304]{1,0:T(8,128)(2,1)}, bf16[192,2304]{1,0:T(8,128)(2,1)S(1)}, u32[]{:S(2)}, u32[]{:S(2)}) collective-permute-start(bf16[192,2304]{1,0:T(8,128)(2,1)} %collective-permute-done.1.refs_11_), channel_id=1, source_target_pairs={{0,3},{1,0},{2,1},{3,2},{4,7},{5,4},{6,5},{7,6},{8,11},{9,8},{10,9... | collective-permute-start | bytes 2654216 | tf_op jit(solution)/shard_map/ppermute | solution.py:648
  60.6 2.2 %collective-permute-start.13 = (bf16[192,2304]{1,0:T(8,128)(2,1)}, bf16[192,2304]{1,0:T(8,128)(2,1)S(1)}, u32[]{:S(2)}, u32[]{:S(2)}) collective-permute-start(bf16[192,2304]{1,0:T(8,128)(2,1)} %collective-permute-done.refs_10_), channel_id=1, source_target_pairs={{0,12},{1,13},{2,14},{3,15},{4,0},{5,1},{6,2},{7,3},{8,4},{9,5},{1... | collective-permute-start | bytes 2654216 | tf_op jit(solution)/shard_map/ppermute | solution.py:648
  62.9 1.1 collective-permute-start.11
  64.0 15.2 %first_application.1 = (bf16[192,2304]{1,0:T(8,128)(2,1)}, bf16[192,2304]{1,0:T(8,128)(2,1)}, bf16[192,2304]{1,0:T(8,128)(2,1)}, bf16[192,2304]{1,0:T(8,128)(2,1...) custom-call(s32[384]{0:T(512)} %convert_element_type.51.refs_0_, ...), custom_call_target="tpu_custom_call" | custom-call | flops 10000000000 | bytes 30000000 | tf_op jit(solution)/shard_map/first_application/pallas_call | solution.py:560
  79.2 3.3 %collective-permute-start.14 = (bf16[192,2304]{1,0:T(8,128)(2,1)}, bf16[192,2304]{1,0:T(8,128)(2,1)S(1)}, u32[]{:S(2)}, u32[]{:S(2)}) collective-permute-start(bf16[192,2304]{1,0:T(8,128)(2,1)} %get-tuple-element.83), channel_id=1, source_target_pairs={{0,12},{1,13},{2,14},{3,15},{4,0},{5,1},{6,2},{7,3},{8,4},{9,5},{1... | collective-permute-start | bytes 2654216 | tf_op jit(solution)/shard_map/ppermute | solution.py:648
  82.5 0.8 copy-done.28
  83.3 0.8 copy-done.29
  84.1 0.9 copy-done.22
  85.0 0.9 copy-done.23
  85.9 14.5 %second_early.1 = (bf16[192,2304]{1,0:T(8,128)(2,1)}, bf16[192,2304]{1,0:T(8,128)(2,1)}, bf16[192,2304]{1,0:T(8,128)(2,1)}, bf16[192,2304]{1,0:T(8,128)(2,1)}, b...) custom-call(s32[384]{0:T(512)} %convert_element_type.51.refs_0_, ...), custom_call_target="tpu_custom_call" | custom-call | flops 10000000000 | bytes 30000000 | tf_op jit(solution)/shard_map/second_early/pallas_call | solution.py:560
  100.4 1.7 %collective-permute-done.14 = bf16[192,2304]{1,0:T(8,128)(2,1)S(1)} collective-permute-done((bf16[192,2304]{1,0:T(8,128)(2,1)}, bf16[192,2304]{1,0:T(8,128)(2,1)S(1)}, u32[]{:S(2)}, u32[]{:S(2)}) %collective-permute-start.14) | collective-permute-done | bytes 884768 | tf_op jit(solution)/shard_map/ppermute | solution.py:648
  102.4 3.7 %collective-permute-start.19 = (bf16[192,2304]{1,0:T(8,128)(2,1)S(1)}, bf16[192,2304]{1,0:T(8,128)(2,1)S(1)}, u32[]{:S(2)}, u32[]{:S(2)}) collective-permute-start(bf16[192,2304]{1,0:T(8,128)(2,1)S(1)} %add_convert_fusion.2), channel_id=1, source_target_pairs={{0,12},{1,13},{2,14},{3,15},{4,0},{5,1},{6,2},{7,3},{8,4},{9,5},{1... | collective-permute-start | bytes 2654216 | tf_op jit(solution)/shard_map/ppermute | solution.py:648
  106.6 1.9 %collective-permute-start.21 = (bf16[192,2304]{1,0:T(8,128)(2,1)}, bf16[192,2304]{1,0:T(8,128)(2,1)S(1)}, u32[]{:S(2)}, u32[]{:S(2)}) collective-permute-start(bf16[192,2304]{1,0:T(8,128)(2,1)} %get-tuple-element.123), channel_id=1, source_target_pairs={{0,1},{1,2},{2,3},{3,0},{4,5},{5,6},{6,7},{7,4},{8,9},{9,10},{10,1... | collective-permute-start | bytes 2654216 | tf_op jit(solution)/shard_map/ppermute | solution.py:648
  108.5 2.0 %collective-permute-start.22 = (bf16[192,2304]{1,0:T(8,128)(2,1)S(1)}, bf16[192,2304]{1,0:T(8,128)(2,1)S(1)}, u32[]{:S(2)}, u32[]{:S(2)}) collective-permute-start(bf16[192,2304]{1,0:T(8,128)(2,1)S(1)} %copy-done.24), channel_id=1, source_target_pairs={{0,4},{1,5},{2,6},{3,7},{4,8},{5,9},{6,10},{7,11},{8,12},{9,13},{1... | collective-permute-start | bytes 2654216 | tf_op jit(solution)/shard_map/ppermute | solution.py:648
  110.5 13.8 %second_late.1 = (bf16[192,2304]{1,0:T(8,128)(2,1)}, bf16[192,2304]{1,0:T(8,128)(2,1)}, bf16[192,2304]{1,0:T(8,128)(2,1)}, bf16[192,2304]{1,0:T(8,128)(2,1)}) custom-call(s32[384]{0:T(512)} %convert_element_type.51.refs_0_, bf16[208,2304]{1,0:T(8,128)(2,1)} %copy-done.3, bf16[208,2304]{1,0:T(8,128)(2,1)} %copy-done.13, bf16[208,2304]{1,0:T(8,128)(2,1)} %copy-done.12, ...), custom_call_target="tpu_custom_call" | custom-call | flops 10000000000 | bytes 30000000 | tf_op jit(solution)/shard_map/second_late/pallas_call | solution.py:560
  124.4 4.4 %collective-permute-done.18.refs_2_ = bf16[192,2304]{1,0:T(8,128)(2,1)S(1)} collective-permute-done((bf16[192,2304]{1,0:T(8,128)(2,1)S(1)}, bf16[192,2304]{1,0:T(8,128)(2,1)S(1)}, u32[]{:S(2)}, u32[]{:S(2)}) %collective-permute-start.18) | collective-permute-done | bytes 884768 | tf_op jit(solution)/shard_map/ppermute | solution.py:648
  128.9 6.8 %collective-permute-done.20 = bf16[192,2304]{1,0:T(8,128)(2,1)S(1)} collective-permute-done((bf16[192,2304]{1,0:T(8,128)(2,1)}, bf16[192,2304]{1,0:T(8,128)(2,1)S(1)}, u32[]{:S(2)}, u32[]{:S(2)}) %collective-permute-start.20) | collective-permute-done | bytes 884768 | tf_op jit(solution)/shard_map/ppermute | solution.py:648
  135.7 1.4 add_convert_fusion
  137.1 3.7 %collective-permute-start.25 = (bf16[192,2304]{1,0:T(8,128)(2,1)S(1)}, bf16[192,2304]{1,0:T(8,128)(2,1)S(1)}, u32[]{:S(2)}, u32[]{:S(2)}) collective-permute-start(bf16[192,2304]{1,0:T(8,128)(2,1)S(1)} %add_convert_fusion), channel_id=1, source_target_pairs={{0,12},{1,13},{2,14},{3,15},{4,0},{5,1},{6,2},{7,3},{8,4},{9,5},{1... | collective-permute-start | bytes 2654216 | tf_op jit(solution)/shard_map/ppermute | solution.py:648
  141.3 1.7 %total.2 = bf16[192,2304]{1,0:T(8,128)(2,1)} custom-call(bf16[192,2304]{1,0:T(8,128)(2,1)S(1)} %copy-done.5, bf16[192,2304]{1,0:T(8,128)(2,1)S(1)} %collective-permute-done.17.refs_1_, bf16[192,2304]{1,0:T(8,128)(2,1)S(1)} %collective-permute-done.18.refs_2_, bf16[192,2304]{1,0:T(8,128)(2,1)S(1)} %collective-permute-done.19.refs_3_, bf16[384,384]{1,0:T(8,128)(2,1)S(1)} %copy-done), custom_call_target="tpu_custom_call" | custom-call | tf_op jit(solution)/shard_map/total/pallas_call | solution.py:626
  143.0 8.3 %collective-permute-done.25.refs_3_ = bf16[192,2304]{1,0:T(8,128)(2,1)S(1)} collective-permute-done((bf16[192,2304]{1,0:T(8,128)(2,1)S(1)}, bf16[192,2304]{1,0:T(8,128)(2,1)S(1)}, u32[]{:S(2)}, u32[]{:S(2)}) %collective-permute-start.25) | collective-permute-done | bytes 884768 | tf_op jit(solution)/shard_map/ppermute | solution.py:648
  151.3 2.9 %collective-permute-done.24.refs_2_ = bf16[192,2304]{1,0:T(8,128)(2,1)S(1)} collective-permute-done((bf16[192,2304]{1,0:T(8,128)(2,1)S(1)}, bf16[192,2304]{1,0:T(8,128)(2,1)S(1)}, u32[]{:S(2)}, u32[]{:S(2)}) %collective-permute-start.24) | collective-permute-done | bytes 884768 | tf_op jit(solution)/shard_map/ppermute | solution.py:648
  154.2 0.7 collective-permute-done.23.refs_1_
  154.9 1.7 %total.3 = bf16[192,2304]{1,0:T(8,128)(2,1)} custom-call(bf16[192,2304]{1,0:T(8,128)(2,1)S(1)} %copy-done.6, bf16[192,2304]{1,0:T(8,128)(2,1)S(1)} %collective-permute-done.23.refs_1_, bf16[192,2304]{1,0:T(8,128)(2,1)S(1)} %collective-permute-done.24.refs_2_, bf16[192,2304]{1,0:T(8,128)(2,1)S(1)} %collective-permute-done.25.refs_3_, bf16[384,384]{1,0:T(8,128)(2,1)S(1)} %copy-done), custom_call_target="tpu_custom_call" | custom-call | tf_op jit(solution)/shard_map/total/pallas_call | solution.py:626
  (92 shorter events, 2.9 us)
Async XLA Ops:
  0.6 13.3 %copy-start.16 = (s32[4,1]{0,1:T(1,128)S(1)}, s32[4,1]{0,1:T(1,128)}, u32[]{:S(2)}) copy-start(s32[4,1]{0,1:T(1,128)} %param.16) | copy-start | bytes 52
  0.6 13.3 %copy-start.17 = (s32[4]{0:T(128)S(1)}, s32[4]{0:T(128)}, u32[]{:S(2)}) copy-start(s32[4]{0:T(128)} %param.15) | copy-start | bytes 52
  0.7 13.3 %copy-start.15 = (s32[4]{0:T(128)S(1)}, s32[4]{0:T(128)}, u32[]{:S(2)}) copy-start(s32[4]{0:T(128)} %param.17) | copy-start | bytes 52
  2.8 9.6 %copy-start.14 = (s32[512,3]{0,1:T(4,128)S(1)}, s32[512,3]{0,1:T(4,128)}, u32[]{:S(2)}) copy-start(s32[512,3]{0,1:T(4,128)} %param.18) | copy-start | bytes 18436
  2.8 14.0 %copy-start.2 = (bf16[384,384]{1,0:T(8,128)(2,1)S(1)}, bf16[384,384]{1,0:T(8,128)(2,1)}, u32[]{:S(2)}) copy-start(bf16[384,384]{1,0:T(8,128)(2,1)} %constant.32.clone.refs_2_.refs_1_) | copy-start | bytes 884740
  2.8 14.0 %copy-start.4 = (bf16[4,48,2304]{2,1,0:T(8,128)(2,1)S(1)}, bf16[4,48,2304]{2,1,0:T(8,128)(2,1)}, u32[]{:S(2)}) copy-start(bf16[4,48,2304]{2,1,0:T(8,128)(2,1)} %param.13) | copy-start | bytes 2654212
  3.5 24.3 %copy-start.8 = (bf16[192,2304]{1,0:T(8,128)(2,1)}, bf16[192,2304]{1,0:T(8,128)(2,1)S(1)}, u32[]{:S(2)}) copy-start(bf16[192,2304]{1,0:T(8,128)(2,1)S(1)} %reorder.3.refs_9_) | copy-start | bytes 2654212
  3.5 15.3 %collective-permute-start = (bf16[192,2304]{1,0:T(8,128)(2,1)S(1)}, bf16[192,2304]{1,0:T(8,128)(2,1)}, u32[]{:S(2)}, u32[]{:S(2)}) collective-permute-start(bf16[192,2304]{1,0:T(8,128)(2,1)S(1)} %reorder.3.refs_9_), channel_id=1, source_target_pairs={{0,1},{1,2},{2,3},{3,0},{4,5},{5,6},{6,7},{7,4},{8,9},{9,10},{10,1... | collective-permute-start | bytes 2654216 | tf_op jit(solution)/shard_map/ppermute | solution.py:648
  5.6 14.4 %collective-permute-start.1 = (bf16[192,2304]{1,0:T(8,128)(2,1)S(1)}, bf16[192,2304]{1,0:T(8,128)(2,1)}, u32[]{:S(2)}, u32[]{:S(2)}) collective-permute-start(bf16[192,2304]{1,0:T(8,128)(2,1)S(1)} %reorder.3.refs_9_), channel_id=1, source_target_pairs={{0,4},{1,5},{2,6},{3,7},{4,8},{5,9},{6,10},{7,11},{8,12},{9,13},{1... | collective-permute-start | bytes 2654216 | tf_op jit(solution)/shard_map/ppermute | solution.py:648
  7.1 15.8 %collective-permute-start.2 = (bf16[192,2304]{1,0:T(8,128)(2,1)S(1)}, bf16[192,2304]{1,0:T(8,128)(2,1)S(1)}, u32[]{:S(2)}, u32[]{:S(2)}) collective-permute-start(bf16[192,2304]{1,0:T(8,128)(2,1)S(1)} %reorder.3.refs_9_), channel_id=1, source_target_pairs={{0,112},{16,0},{32,16},{48,32},{64,48},{80,64},{96,80},{112,96},{1... | collective-permute-start | bytes 2654216 | tf_op jit(solution)/shard_map/ppermute | solution.py:656
  17.6 26.0 %copy-start.3 = (bf16[208,2304]{1,0:T(8,128)(2,1)}, bf16[208,2304]{1,0:T(8,128)(2,1)S(1)}, u32[]{:S(2)}) copy-start(bf16[208,2304]{1,0:T(8,128)(2,1)S(1)} %reorder.2.refs_1_) | copy-start | bytes 2875396
  22.9 15.1 %copy-start.21 = (bf16[192,2304]{1,0:T(8,128)(2,1)}, bf16[192,2304]{1,0:T(8,128)(2,1)S(1)}, u32[]{:S(2)}) copy-start(bf16[192,2304]{1,0:T(8,128)(2,1)S(1)} %collective-permute-done.2.refs_16_) | copy-start | bytes 2654212
  22.9 15.0 %collective-permute-start.3 = (bf16[208,2304]{1,0:T(8,128)(2,1)S(1)}, bf16[208,2304]{1,0:T(8,128)(2,1)S(1)}, u32[]{:S(2)}, u32[]{:S(2)}) collective-permute-start(bf16[208,2304]{1,0:T(8,128)(2,1)S(1)} %reorder.2.refs_1_), channel_id=1, source_target_pairs={{0,1},{1,2},{2,3},{3,0},{4,5},{5,6},{6,7},{7,4},{8,9},{9,10},{10,1... | collective-permute-start | bytes 2875400 | tf_op jit(solution)/shard_map/ppermute | solution.py:648
  22.9 15.0 %collective-permute-start.4 = (bf16[208,2304]{1,0:T(8,128)(2,1)S(1)}, bf16[208,2304]{1,0:T(8,128)(2,1)S(1)}, u32[]{:S(2)}, u32[]{:S(2)}) collective-permute-start(bf16[208,2304]{1,0:T(8,128)(2,1)S(1)} %reorder.2.refs_1_), channel_id=1, source_target_pairs={{0,4},{1,5},{2,6},{3,7},{4,8},{5,9},{6,10},{7,11},{8,12},{9,13},{1... | collective-permute-start | bytes 2875400 | tf_op jit(solution)/shard_map/ppermute | solution.py:648
  23.0 15.1 %collective-permute-start.5 = (bf16[208,2304]{1,0:T(8,128)(2,1)S(1)}, bf16[208,2304]{1,0:T(8,128)(2,1)S(1)}, u32[]{:S(2)}, u32[]{:S(2)}) collective-permute-start(bf16[208,2304]{1,0:T(8,128)(2,1)S(1)} %reorder.2.refs_1_), channel_id=1, source_target_pairs={{0,112},{16,0},{32,16},{48,32},{64,48},{80,64},{96,80},{112,96},{1... | collective-permute-start | bytes 2875400 | tf_op jit(solution)/shard_map/ppermute | solution.py:656
  38.0 18.9 %copy-start.13 = (bf16[208,2304]{1,0:T(8,128)(2,1)}, bf16[208,2304]{1,0:T(8,128)(2,1)S(1)}, u32[]{:S(2)}) copy-start(bf16[208,2304]{1,0:T(8,128)(2,1)S(1)} %collective-permute-done.3.refs_2_) | copy-start | bytes 2875396
  38.0 18.4 %copy-start.12 = (bf16[208,2304]{1,0:T(8,128)(2,1)}, bf16[208,2304]{1,0:T(8,128)(2,1)S(1)}, u32[]{:S(2)}) copy-start(bf16[208,2304]{1,0:T(8,128)(2,1)S(1)} %collective-permute-done.4.refs_3_) | copy-start | bytes 2875396
  38.1 18.8 %collective-permute-start.8 = (bf16[208,2304]{1,0:T(8,128)(2,1)S(1)}, bf16[208,2304]{1,0:T(8,128)(2,1)S(1)}, u32[]{:S(2)}, u32[]{:S(2)}) collective-permute-start(bf16[208,2304]{1,0:T(8,128)(2,1)S(1)} %collective-permute-done.4.refs_3_), channel_id=1, source_target_pairs={{0,3},{1,0},{2,1},{3,2},{4,7},{5,4},{6,5},{7,6},{8,11},{9,8},{10,9... | collective-permute-start | bytes 2875400 | tf_op jit(solution)/shard_map/ppermute | solution.py:648
  41.3 16.3 %collective-permute-start.9 = (bf16[208,2304]{1,0:T(8,128)(2,1)S(1)}, bf16[208,2304]{1,0:T(8,128)(2,1)S(1)}, u32[]{:S(2)}, u32[]{:S(2)}) collective-permute-start(bf16[208,2304]{1,0:T(8,128)(2,1)S(1)} %collective-permute-done.3.refs_2_), channel_id=1, source_target_pairs={{0,12},{1,13},{2,14},{3,15},{4,0},{5,1},{6,2},{7,3},{8,4},{9,5},{1... | collective-permute-start | bytes 2875400 | tf_op jit(solution)/shard_map/ppermute | solution.py:648
  41.4 15.1 %collective-permute-start.7 = (bf16[112,2304]{1,0:T(8,128)(2,1)S(1)}, bf16[112,2304]{1,0:T(8,128)(2,1)S(1)}, u32[]{:S(2)}, u32[]{:S(2)}) collective-permute-start(bf16[112,2304]{1,0:T(8,128)(2,1)S(1)} %slice.36), channel_id=1, source_target_pairs={{0,1},{1,2},{2,3},{3,0},{4,5},{5,6},{6,7},{7,4},{8,9},{9,10},{10,1... | collective-permute-start | bytes 1548296 | tf_op jit(solution)/shard_map/ppermute | solution.py:648
  41.5 14.4 %collective-permute-start.6 = (bf16[96,2304]{1,0:T(8,128)(2,1)S(1)}, bf16[96,2304]{1,0:T(8,128)(2,1)S(1)}, u32[]{:S(2)}, u32[]{:S(2)}) collective-permute-start(bf16[96,2304]{1,0:T(8,128)(2,1)S(1)} %slice.35), channel_id=1, source_target_pairs={{0,4},{1,5},{2,6},{3,7},{4,8},{5,9},{6,10},{7,11},{8,12},{9,13},{1... | collective-permute-start | bytes 1327112 | tf_op jit(solution)/shard_map/ppermute | solution.py:648
  56.4 7.6 %copy-start.26 = (bf16[112,2304]{1,0:T(8,128)(2,1)}, bf16[112,2304]{1,0:T(8,128)(2,1)S(1)}, u32[]{:S(2)}) copy-start(bf16[112,2304]{1,0:T(8,128)(2,1)S(1)} %collective-permute-done.7.refs_5_) | copy-start | bytes 1548292
  56.9 7.1 %copy-start.18 = (bf16[208,2304]{1,0:T(8,128)(2,1)}, bf16[208,2304]{1,0:T(8,128)(2,1)S(1)}, u32[]{:S(2)}) copy-start(bf16[208,2304]{1,0:T(8,128)(2,1)S(1)} %collective-permute-done.8.refs_6_) | copy-start | bytes 2875396
  57.6 6.4 %copy-start.19 = (bf16[208,2304]{1,0:T(8,128)(2,1)}, bf16[208,2304]{1,0:T(8,128)(2,1)S(1)}, u32[]{:S(2)}) copy-start(bf16[208,2304]{1,0:T(8,128)(2,1)S(1)} %collective-permute-done.9.refs_7_) | copy-start | bytes 2875396
  58.4 25.6 %collective-permute-start.12 = (bf16[192,2304]{1,0:T(8,128)(2,1)}, bf16[192,2304]{1,0:T(8,128)(2,1)S(1)}, u32[]{:S(2)}, u32[]{:S(2)}) collective-permute-start(bf16[192,2304]{1,0:T(8,128)(2,1)} %collective-permute-done.1.refs_11_), channel_id=1, source_target_pairs={{0,3},{1,0},{2,1},{3,2},{4,7},{5,4},{6,5},{7,6},{8,11},{9,8},{10,9... | collective-permute-start | bytes 2654216 | tf_op jit(solution)/shard_map/ppermute | solution.py:648
  60.6 24.4 %collective-permute-start.13 = (bf16[192,2304]{1,0:T(8,128)(2,1)}, bf16[192,2304]{1,0:T(8,128)(2,1)S(1)}, u32[]{:S(2)}, u32[]{:S(2)}) collective-permute-start(bf16[192,2304]{1,0:T(8,128)(2,1)} %collective-permute-done.refs_10_), channel_id=1, source_target_pairs={{0,12},{1,13},{2,14},{3,15},{4,0},{5,1},{6,2},{7,3},{8,4},{9,5},{1... | collective-permute-start | bytes 2654216 | tf_op jit(solution)/shard_map/ppermute | solution.py:648
  62.9 19.7 %collective-permute-start.10 = (bf16[96,2304]{1,0:T(8,128)(2,1)S(1)}, bf16[96,2304]{1,0:T(8,128)(2,1)S(1)}, u32[]{:S(2)}, u32[]{:S(2)}) collective-permute-start(bf16[96,2304]{1,0:T(8,128)(2,1)S(1)} %slice.31), channel_id=1, source_target_pairs={{0,4},{1,5},{2,6},{3,7},{4,8},{5,9},{6,10},{7,11},{8,12},{9,13},{1... | collective-permute-start | bytes 1327112 | tf_op jit(solution)/shard_map/ppermute | solution.py:648
  62.9 20.5 %collective-permute-start.11 = (bf16[96,2304]{1,0:T(8,128)(2,1)S(1)}, bf16[96,2304]{1,0:T(8,128)(2,1)S(1)}, u32[]{:S(2)}, u32[]{:S(2)}) collective-permute-start(bf16[96,2304]{1,0:T(8,128)(2,1)S(1)} %slice.32), channel_id=1, source_target_pairs={{0,1},{1,2},{2,3},{3,0},{4,5},{5,6},{6,7},{7,4},{8,9},{9,10},{10,1... | collective-permute-start | bytes 1327112 | tf_op jit(solution)/shard_map/ppermute | solution.py:648
  79.2 22.9 %collective-permute-start.14 = (bf16[192,2304]{1,0:T(8,128)(2,1)}, bf16[192,2304]{1,0:T(8,128)(2,1)S(1)}, u32[]{:S(2)}, u32[]{:S(2)}) collective-permute-start(bf16[192,2304]{1,0:T(8,128)(2,1)} %get-tuple-element.83), channel_id=1, source_target_pairs={{0,12},{1,13},{2,14},{3,15},{4,0},{5,1},{6,2},{7,3},{8,4},{9,5},{1... | collective-permute-start | bytes 2654216 | tf_op jit(solution)/shard_map/ppermute | solution.py:648
  83.3 18.8 %collective-permute-start.15 = (bf16[192,2304]{1,0:T(8,128)(2,1)}, bf16[192,2304]{1,0:T(8,128)(2,1)S(1)}, u32[]{:S(2)}, u32[]{:S(2)}) collective-permute-start(bf16[192,2304]{1,0:T(8,128)(2,1)} %get-tuple-element.84), channel_id=1, source_target_pairs={{0,1},{1,2},{2,3},{3,0},{4,5},{5,6},{6,7},{7,4},{8,9},{9,10},{10,1... | collective-permute-start | bytes 2654216 | tf_op jit(solution)/shard_map/ppermute | solution.py:648
  84.1 18.1 %collective-permute-start.16 = (bf16[192,2304]{1,0:T(8,128)(2,1)}, bf16[192,2304]{1,0:T(8,128)(2,1)S(1)}, u32[]{:S(2)}, u32[]{:S(2)}) collective-permute-start(bf16[192,2304]{1,0:T(8,128)(2,1)} %get-tuple-element.85), channel_id=1, source_target_pairs={{0,4},{1,5},{2,6},{3,7},{4,8},{5,9},{6,10},{7,11},{8,12},{9,13},{1... | collective-permute-start | bytes 2654216 | tf_op jit(solution)/shard_map/ppermute | solution.py:648
  85.0 17.1 %collective-permute-start.17 = (bf16[192,2304]{1,0:T(8,128)(2,1)}, bf16[192,2304]{1,0:T(8,128)(2,1)S(1)}, u32[]{:S(2)}, u32[]{:S(2)}) collective-permute-start(bf16[192,2304]{1,0:T(8,128)(2,1)} %get-tuple-element.86), channel_id=1, source_target_pairs={{0,16},{16,32},{32,48},{48,64},{64,80},{80,96},{96,112},{112,0},{1... | collective-permute-start | bytes 2654216 | tf_op jit(solution)/shard_map/ppermute | solution.py:656
  85.9 16.2 %copy-start.11 = (bf16[192,2304]{1,0:T(8,128)(2,1)S(1)}, bf16[192,2304]{1,0:T(8,128)(2,1)}, u32[]{:S(2)}) copy-start(bf16[192,2304]{1,0:T(8,128)(2,1)} %get-tuple-element.120) | copy-start | bytes 2654212
  100.4 5.6 %copy-start.9 = (bf16[192,2304]{1,0:T(8,128)(2,1)S(1)}, bf16[192,2304]{1,0:T(8,128)(2,1)}, u32[]{:S(2)}) copy-start(bf16[192,2304]{1,0:T(8,128)(2,1)} %get-tuple-element.117) | copy-start | bytes 2654212
  102.4 6.2 %copy-start.24 = (bf16[192,2304]{1,0:T(8,128)(2,1)S(1)}, bf16[192,2304]{1,0:T(8,128)(2,1)}, u32[]{:S(2)}) copy-start(bf16[192,2304]{1,0:T(8,128)(2,1)} %get-tuple-element.124) | copy-start | bytes 2654212
  102.4 22.0 %collective-permute-start.19 = (bf16[192,2304]{1,0:T(8,128)(2,1)S(1)}, bf16[192,2304]{1,0:T(8,128)(2,1)S(1)}, u32[]{:S(2)}, u32[]{:S(2)}) collective-permute-start(bf16[192,2304]{1,0:T(8,128)(2,1)S(1)} %add_convert_fusion.2), channel_id=1, source_target_pairs={{0,12},{1,13},{2,14},{3,15},{4,0},{5,1},{6,2},{7,3},{8,4},{9,5},{1... | collective-permute-start | bytes 2654216 | tf_op jit(solution)/shard_map/ppermute | solution.py:648
  106.4 22.4 %collective-permute-start.18 = (bf16[192,2304]{1,0:T(8,128)(2,1)S(1)}, bf16[192,2304]{1,0:T(8,128)(2,1)S(1)}, u32[]{:S(2)}, u32[]{:S(2)}) collective-permute-start(bf16[192,2304]{1,0:T(8,128)(2,1)S(1)} %add_convert_fusion.3), channel_id=1, source_target_pairs={{0,3},{1,0},{2,1},{3,2},{4,7},{5,4},{6,5},{7,6},{8,11},{9,8},{10,9... | collective-permute-start | bytes 2654216 | tf_op jit(solution)/shard_map/ppermute | solution.py:648
  106.5 29.2 %collective-permute-start.20 = (bf16[192,2304]{1,0:T(8,128)(2,1)}, bf16[192,2304]{1,0:T(8,128)(2,1)S(1)}, u32[]{:S(2)}, u32[]{:S(2)}) collective-permute-start(bf16[192,2304]{1,0:T(8,128)(2,1)} %get-tuple-element.122), channel_id=1, source_target_pairs={{0,12},{1,13},{2,14},{3,15},{4,0},{5,1},{6,2},{7,3},{8,4},{9,5},{1... | collective-permute-start | bytes 2654216 | tf_op jit(solution)/shard_map/ppermute | solution.py:648
  106.6 29.1 %collective-permute-start.21 = (bf16[192,2304]{1,0:T(8,128)(2,1)}, bf16[192,2304]{1,0:T(8,128)(2,1)S(1)}, u32[]{:S(2)}, u32[]{:S(2)}) collective-permute-start(bf16[192,2304]{1,0:T(8,128)(2,1)} %get-tuple-element.123), channel_id=1, source_target_pairs={{0,1},{1,2},{2,3},{3,0},{4,5},{5,6},{6,7},{7,4},{8,9},{9,10},{10,1... | collective-permute-start | bytes 2654216 | tf_op jit(solution)/shard_map/ppermute | solution.py:648
  108.5 27.1 %collective-permute-start.22 = (bf16[192,2304]{1,0:T(8,128)(2,1)S(1)}, bf16[192,2304]{1,0:T(8,128)(2,1)S(1)}, u32[]{:S(2)}, u32[]{:S(2)}) collective-permute-start(bf16[192,2304]{1,0:T(8,128)(2,1)S(1)} %copy-done.24), channel_id=1, source_target_pairs={{0,4},{1,5},{2,6},{3,7},{4,8},{5,9},{6,10},{7,11},{8,12},{9,13},{1... | collective-permute-start | bytes 2654216 | tf_op jit(solution)/shard_map/ppermute | solution.py:648
  124.4 16.4 %copy-start.10 = (bf16[192,2304]{1,0:T(8,128)(2,1)S(1)}, bf16[192,2304]{1,0:T(8,128)(2,1)}, u32[]{:S(2)}) copy-start(bf16[192,2304]{1,0:T(8,128)(2,1)} %get-tuple-element.129) | copy-start | bytes 2654212
  137.1 4.2 %copy-start.25 = (bf16[192,2304]{1,0:T(8,128)(2,1)S(1)}, bf16[192,2304]{1,0:T(8,128)(2,1)}, u32[]{:S(2)}) copy-start(bf16[192,2304]{1,0:T(8,128)(2,1)} %get-tuple-element.128) | copy-start | bytes 2654212
  137.1 4.2 %copy-start = (bf16[384,384]{1,0:T(8,128)(2,1)S(1)}, bf16[384,384]{1,0:T(8,128)(2,1)}, u32[]{:S(2)}) copy-start(bf16[384,384]{1,0:T(8,128)(2,1)} %constant.33.clone.refs_4_) | copy-start | bytes 884740
  137.1 4.2 %copy-start.5 = (bf16[192,2304]{1,0:T(8,128)(2,1)S(1)}, bf16[192,2304]{1,0:T(8,128)(2,1)}, u32[]{:S(2)}) copy-start(bf16[192,2304]{1,0:T(8,128)(2,1)} %get-tuple-element.107.refs_0_) | copy-start | bytes 2654212
  137.1 14.2 %collective-permute-start.25 = (bf16[192,2304]{1,0:T(8,128)(2,1)S(1)}, bf16[192,2304]{1,0:T(8,128)(2,1)S(1)}, u32[]{:S(2)}, u32[]{:S(2)}) collective-permute-start(bf16[192,2304]{1,0:T(8,128)(2,1)S(1)} %add_convert_fusion), channel_id=1, source_target_pairs={{0,12},{1,13},{2,14},{3,15},{4,0},{5,1},{6,2},{7,3},{8,4},{9,5},{1... | collective-permute-start | bytes 2654216 | tf_op jit(solution)/shard_map/ppermute | solution.py:648
  141.1 13.8 %copy-start.6 = (bf16[192,2304]{1,0:T(8,128)(2,1)S(1)}, bf16[192,2304]{1,0:T(8,128)(2,1)}, u32[]{:S(2)}) copy-start(bf16[192,2304]{1,0:T(8,128)(2,1)} %get-tuple-element.127.refs_0_) | copy-start | bytes 2654212
  141.1 13.1 %collective-permute-start.24 = (bf16[192,2304]{1,0:T(8,128)(2,1)S(1)}, bf16[192,2304]{1,0:T(8,128)(2,1)S(1)}, u32[]{:S(2)}, u32[]{:S(2)}) collective-permute-start(bf16[192,2304]{1,0:T(8,128)(2,1)S(1)} %add_convert_fusion.1), channel_id=1, source_target_pairs={{0,3},{1,0},{2,1},{3,2},{4,7},{5,4},{6,5},{7,6},{8,11},{9,8},{10,9... | collective-permute-start | bytes 2654216 | tf_op jit(solution)/shard_map/ppermute | solution.py:648
  141.2 13.7 %collective-permute-start.23 = (bf16[192,2304]{1,0:T(8,128)(2,1)S(1)}, bf16[192,2304]{1,0:T(8,128)(2,1)S(1)}, u32[]{:S(2)}, u32[]{:S(2)}) collective-permute-start(bf16[192,2304]{1,0:T(8,128)(2,1)S(1)} %copy-done.25), channel_id=1, source_target_pairs={{0,16},{16,32},{32,48},{48,64},{64,80},{80,96},{96,112},{112,0},{1... | collective-permute-start | bytes 2654216 | tf_op jit(solution)/shard_map/ppermute | solution.py:656
  (8 other events, 10.5 us)

commit v2 on v1

--- a/solution.py
+++ b/solution.py
@@ -576,7 +576,7 @@
             pltpu.SemaphoreType.DMA((N_TABLES,)),
             pltpu.SemaphoreType.DMA((SOURCES,)),
         ],
-        compiler_params=pltpu.CompilerParams(vmem_limit_bytes=56 * 1024 * 1024),
+        compiler_params=pltpu.CompilerParams(vmem_limit_bytes=62 * 1024 * 1024),
         cost_estimate=pl.CostEstimate(
             flops=10_000_000_000, bytes_accessed=30_000_000, transcendentals=0
         ),

time: 157 us -> 164 us (1.045); the launches traced: 157 us -> 166 us
  starting transfers between devices: 38.4 us -> 50.3 us
  other arithmetic: 4.79 us -> 11.2 us
  waiting for transfers between devices: 53.5 us -> 47.3 us
  Pallas kernels: 50.1 us -> 48 us
    ppermute x22, starting transfers between devices: 29.3 us -> 41.2 us  [move(): return lax.ppermute(block, ('region', 'sub'), pairs)]
    ppermute x22, waiting for transfers between devices: 49.8 us -> 41.1 us  [move(): return lax.ppermute(block, ('region', 'sub'), pairs)]
    convert_element_type x2, other arithmetic: 0.73 us -> 4.52 us  [merge(): m01 = (c01.astype(F32) + r31.astype(F32) + r11.astype(F32)).astype(BF16)]
    pallas_call x3, Pallas kernels: 43.5 us -> 40.4 us  [exchange(): pl.pallas_call(kernel, out_shape=outs, in_specs=[smem] + [any_space] * (l...]
    convert_element_type x2, other arithmetic: 1.58 us -> 4.19 us  [merge(): m10 = (c10.astype(F32) + r13.astype(F32)).astype(BF16)]
    ppermute x4, waiting for transfers between devices: 3.73 us -> 6.19 us  [move(): return lax.ppermute(block, 'region', pairs)]
    unnamed x61 -> x49, local copies, waits for them, and re-layouts: 5.75 us -> 5.12 us
  transfers between devices with their start and end apart: 26 -> 26, of which waited for: 15 -> 14; matrix products, arithmetic and copies ran while one was open for 4% -> 6% of each run, Pallas kernels for 30% -> 27%
where the time goes in v2:
time: 164 us; the launch traced here: 166 us
  starting transfers between devices  50.3 us (31%)
  Pallas kernels  48 us (29%)
  waiting for transfers between devices  47.3 us (29%)
  other arithmetic  11.2 us (7%)
  local copies, waits for them, and re-layouts  8.21 us (5%)
    ppermute x22, starting transfers between devices, move(): return lax.ppermute(block, ('region', 'sub'), pairs)  41.2 us
    ppermute x22, waiting for transfers between devices, move(): return lax.ppermute(block, ('region', 'sub'), pairs)  41.1 us
    pallas_call x3, Pallas kernels, exchange(): pl.pallas_call(kernel, out_shape=outs, in_specs=[smem] + [any_space] * (l...  40.4 us
    ppermute x4, starting transfers between devices, move(): return lax.ppermute(block, 'region', pairs)  9.08 us
    ppermute x4, waiting for transfers between devices, move(): return lax.ppermute(block, 'region', pairs)  6.19 us
    unnamed x49, local copies, waits for them, and re-layouts  5.12 us
    convert_element_type x2, other arithmetic, merge(): m01 = (c01.astype(F32) + r31.astype(F32) + r11.astype(F32)).astype(BF16)  4.52 us
    pallas_call x2, Pallas kernels, total(): pl.pallas_call(total_kernel, grid=(2,), out_shape=jax.ShapeDtypeStruct((S...  4.46 us
  transfers between devices with their start and end apart: 26, of which 14 were waited for; matrix products, arithmetic and copies ran while one was open for 6% of the time, Pallas kernels for 27%

profile of v2, /device:TPU:0, one launch (start us, length us, event | category | flops | bytes accessed | tf_op | source)
XLA Modules:
  0.0 166.0 jit_solution(6581407473924323088)
XLA Ops:
  0.7 1.0 copy-done.1
  1.6 1.2 copy-done.7
  2.8 0.7 reorder.3.refs_9_
  3.5 2.1 %collective-permute-start = (bf16[192,2304]{1,0:T(8,128)(2,1)S(1)}, bf16[192,2304]{1,0:T(8,128)(2,1)}, u32[]{:S(2)}, u32[]{:S(2)}) collective-permute-start(bf16[192,2304]{1,0:T(8,128)(2,1)S(1)} %reorder.3.refs_9_), channel_id=1, source_target_pairs={{0,1},{1,2},{2,3},{3,0},{4,5},{5,6},{6,7},{7,4},{8,9},{9,10},{10,1... | collective-permute-start | bytes 2654216 | tf_op jit(solution)/shard_map/ppermute | solution.py:648
  5.6 1.5 collective-permute-start.1
  7.1 5.3 %collective-permute-start.2 = (bf16[192,2304]{1,0:T(8,128)(2,1)S(1)}, bf16[192,2304]{1,0:T(8,128)(2,1)S(1)}, u32[]{:S(2)}, u32[]{:S(2)}) collective-permute-start(bf16[192,2304]{1,0:T(8,128)(2,1)S(1)} %reorder.3.refs_9_), channel_id=1, source_target_pairs={{0,112},{16,0},{32,16},{48,32},{64,48},{80,64},{96,80},{112,96},{1... | collective-permute-start | bytes 2654216 | tf_op jit(solution)/shard_map/ppermute | solution.py:656
  12.5 0.8 reshape.20.refs_2_
  13.3 0.7 pad_add_fusion.refs_0_
  14.6 1.7 %plan.1 = s32[64]{0:T(128)} custom-call(s32[3]{0:T(128)} %pad_add_fusion.refs_0_, s32[12]{0:T(128)} %pad_add_fusion.1.refs_1_, s32[1536]{0:T(1024)} %reshape.20.refs_2_, s32[112]{0:T(128)} %constant.34.clone.refs_3_), custom_call_target="tpu_custom_call" | custom-call | tf_op jit(solution)/shard_map/plan/pallas_call | solution.py:682
  17.0 0.7 reorder.2.refs_1_
  17.7 1.2 collective-permute-done.refs_10_
  18.9 1.1 collective-permute-done.1.refs_11_
  20.0 3.0 %collective-permute-done.2.refs_16_ = bf16[192,2304]{1,0:T(8,128)(2,1)S(1)} collective-permute-done((bf16[192,2304]{1,0:T(8,128)(2,1)S(1)}, bf16[192,2304]{1,0:T(8,128)(2,1)S(1)}, u32[]{:S(2)}, u32[]{:S(2)}) %collective-permute-start.2) | collective-permute-done | bytes 884768 | tf_op jit(solution)/shard_map/ppermute | solution.py:656
  22.9 0.9 copy-done.20
  23.9 3.8 %collective-permute-start.5 = (bf16[208,2304]{1,0:T(8,128)(2,1)S(1)}, bf16[208,2304]{1,0:T(8,128)(2,1)}, u32[]{:S(2)}, u32[]{:S(2)}) collective-permute-start(bf16[208,2304]{1,0:T(8,128)(2,1)S(1)} %reorder.2.refs_1_), channel_id=1, source_target_pairs={{0,112},{16,0},{32,16},{48,32},{64,48},{80,64},{96,80},{112,96},{1... | collective-permute-start | bytes 2875400 | tf_op jit(solution)/shard_map/ppermute | solution.py:656
  27.6 1.0 slice.31
  28.7 1.0 slice.32
  29.7 9.2 %collective-permute-done.3.refs_2_ = bf16[208,2304]{1,0:T(8,128)(2,1)S(1)} collective-permute-done((bf16[208,2304]{1,0:T(8,128)(2,1)S(1)}, bf16[208,2304]{1,0:T(8,128)(2,1)S(1)}, u32[]{:S(2)}, u32[]{:S(2)}) %collective-permute-start.3) | collective-permute-done | bytes 958496 | tf_op jit(solution)/shard_map/ppermute | solution.py:648
  39.0 3.1 %collective-permute-start.8 = (bf16[208,2304]{1,0:T(8,128)(2,1)S(1)}, bf16[208,2304]{1,0:T(8,128)(2,1)S(1)}, u32[]{:S(2)}, u32[]{:S(2)}) collective-permute-start(bf16[208,2304]{1,0:T(8,128)(2,1)S(1)} %collective-permute-done.4.refs_3_), channel_id=1, source_target_pairs={{0,3},{1,0},{2,1},{3,2},{4,7},{5,4},{6,5},{7,6},{8,11},{9,8},{10,9... | collective-permute-start | bytes 2875400 | tf_op jit(solution)/shard_map/ppermute | solution.py:648
  42.3 2.1 %collective-permute-start.6 = (bf16[96,2304]{1,0:T(8,128)(2,1)S(1)}, bf16[96,2304]{1,0:T(8,128)(2,1)S(1)}, u32[]{:S(2)}, u32[]{:S(2)}) collective-permute-start(bf16[96,2304]{1,0:T(8,128)(2,1)S(1)} %slice.35), channel_id=1, source_target_pairs={{0,4},{1,5},{2,6},{3,7},{4,8},{5,9},{6,10},{7,11},{8,12},{9,13},{1... | collective-permute-start | bytes 1327112 | tf_op jit(solution)/shard_map/ppermute | solution.py:648
  44.4 12.3 %collective-permute-done.6.refs_4_ = bf16[96,2304]{1,0:T(8,128)(2,1)S(1)} collective-permute-done((bf16[96,2304]{1,0:T(8,128)(2,1)S(1)}, bf16[96,2304]{1,0:T(8,128)(2,1)S(1)}, u32[]{:S(2)}, u32[]{:S(2)}) %collective-permute-start.6) | collective-permute-done | bytes 442400 | tf_op jit(solution)/shard_map/ppermute | solution.py:648
  56.7 0.7 collective-permute-done.7.refs_5_
  57.9 0.6 collective-permute-done.9.refs_7_
  58.9 0.7 copy-done.19
  60.3 2.5 %collective-permute-start.12 = (bf16[192,2304]{1,0:T(8,128)(2,1)}, bf16[192,2304]{1,0:T(8,128)(2,1)}, u32[]{:S(2)}, u32[]{:S(2)}) collective-permute-start(bf16[192,2304]{1,0:T(8,128)(2,1)} %collective-permute-done.1.refs_11_), channel_id=1, source_target_pairs={{0,3},{1,0},{2,1},{3,2},{4,7},{5,4},{6,5},{7,6},{8,11},{9,8},{10,9... | collective-permute-start | bytes 2654216 | tf_op jit(solution)/shard_map/ppermute | solution.py:648
  62.8 1.6 collective-permute-start.13
  64.8 0.9 collective-permute-start.11
  65.6 11.9 %first_application.1 = (bf16[192,2304]{1,0:T(8,128)(2,1)}, bf16[192,2304]{1,0:T(8,128)(2,1)}, bf16[192,2304]{1,0:T(8,128)(2,1)}, bf16[192,2304]{1,0:T(8,128)(2,1...) custom-call(s32[384]{0:T(512)} %convert_element_type.51.refs_0_, ...), custom_call_target="tpu_custom_call" | custom-call | flops 10000000000 | bytes 30000000 | tf_op jit(solution)/shard_map/first_application/pallas_call | solution.py:560
  77.6 9.9 %collective-permute-start.14 = (bf16[192,2304]{1,0:T(8,128)(2,1)}, bf16[192,2304]{1,0:T(8,128)(2,1)S(1)}, u32[]{:S(2)}, u32[]{:S(2)}) collective-permute-start(bf16[192,2304]{1,0:T(8,128)(2,1)} %get-tuple-element.83), channel_id=1, source_target_pairs={{0,12},{1,13},{2,14},{3,15},{4,0},{5,1},{6,2},{7,3},{8,4},{9,5},{1... | collective-permute-start | bytes 2654216 | tf_op jit(solution)/shard_map/ppermute | solution.py:648
  87.8 15.1 %second_early.1 = (bf16[192,2304]{1,0:T(8,128)(2,1)}, bf16[192,2304]{1,0:T(8,128)(2,1)}, bf16[192,2304]{1,0:T(8,128)(2,1)}, bf16[192,2304]{1,0:T(8,128)(2,1)}, b...) custom-call(s32[384]{0:T(512)} %convert_element_type.51.refs_0_, ...), custom_call_target="tpu_custom_call" | custom-call | flops 10000000000 | bytes 30000000 | tf_op jit(solution)/shard_map/second_early/pallas_call | solution.py:560
  103.0 0.9 copy-done.10
  103.8 2.6 %add_convert_fusion.2 = bf16[192,2304]{1,0:T(8,128)(2,1)} fusion(bf16[192,2304]{1,0:T(8,128)(2,1)} %collective-permute-done.15, bf16[192,2304]{1,0:T(8,128)(2,1)} %get-tuple-element.120), kind=kLoop, calls=%fused_computation.2 | loop fusion | flops 1769472 | bytes 2654208 | tf_op jit(solution)/shard_map/convert_element_type | solution.py:707
  106.4 3.1 %collective-permute-start.19 = (bf16[192,2304]{1,0:T(8,128)(2,1)}, bf16[192,2304]{1,0:T(8,128)(2,1)S(1)}, u32[]{:S(2)}, u32[]{:S(2)}) collective-permute-start(bf16[192,2304]{1,0:T(8,128)(2,1)} %add_convert_fusion.2), channel_id=1, source_target_pairs={{0,12},{1,13},{2,14},{3,15},{4,0},{5,1},{6,2},{7,3},{8,4},{9,5},{1... | collective-permute-start | bytes 2654216 | tf_op jit(solution)/shard_map/ppermute | solution.py:648
  109.5 2.7 %add_convert_fusion.3 = bf16[192,2304]{1,0:T(8,128)(2,1)} fusion(bf16[192,2304]{1,0:T(8,128)(2,1)} %copy-done.10, bf16[192,2304]{1,0:T(8,128)(2,1)} %collective-permute-done.16, bf16[192,2304]{1,0:T(8,128)(2,1)S(1)} %copy-done.9), kind=kLoop, calls=%fused_computation.3 | loop fusion | flops 2654208 | bytes 3538944 | tf_op jit(solution)/shard_map/convert_element_type | solution.py:706
  112.2 4.0 %collective-permute-start.18 = (bf16[192,2304]{1,0:T(8,128)(2,1)}, bf16[192,2304]{1,0:T(8,128)(2,1)}, u32[]{:S(2)}, u32[]{:S(2)}) collective-permute-start(bf16[192,2304]{1,0:T(8,128)(2,1)} %add_convert_fusion.3), channel_id=1, source_target_pairs={{0,3},{1,0},{2,1},{3,2},{4,7},{5,4},{6,5},{7,6},{8,11},{9,8},{10,9... | collective-permute-start | bytes 2654216 | tf_op jit(solution)/shard_map/ppermute | solution.py:648
  116.1 2.0 %collective-permute-start.22 = (bf16[192,2304]{1,0:T(8,128)(2,1)}, bf16[192,2304]{1,0:T(8,128)(2,1)}, u32[]{:S(2)}, u32[]{:S(2)}) collective-permute-start(bf16[192,2304]{1,0:T(8,128)(2,1)} %get-tuple-element.124), channel_id=1, source_target_pairs={{0,4},{1,5},{2,6},{3,7},{4,8},{5,9},{6,10},{7,11},{8,12},{9,13},{1... | collective-permute-start | bytes 2654216 | tf_op jit(solution)/shard_map/ppermute | solution.py:648
  118.2 13.4 %second_late.1 = (bf16[192,2304]{1,0:T(8,128)(2,1)}, bf16[192,2304]{1,0:T(8,128)(2,1)}, bf16[192,2304]{1,0:T(8,128)(2,1)}, bf16[192,2304]{1,0:T(8,128)(2,1)}) custom-call(s32[384]{0:T(512)} %convert_element_type.51.refs_0_, bf16[208,2304]{1,0:T(8,128)(2,1)} %copy-done.3, bf16[208,2304]{1,0:T(8,128)(2,1)} %copy-done.13, bf16[208,2304]{1,0:T(8,128)(2,1)} %copy-done.12, ...), custom_call_target="tpu_custom_call" | custom-call | flops 10000000000 | bytes 30000000 | tf_op jit(solution)/shard_map/second_late/pallas_call | solution.py:560
  131.6 0.7 collective-permute-done.18.refs_2_
  132.3 7.0 %collective-permute-done.20 = bf16[192,2304]{1,0:T(8,128)(2,1)} collective-permute-done((bf16[192,2304]{1,0:T(8,128)(2,1)}, bf16[192,2304]{1,0:T(8,128)(2,1)}, u32[]{:S(2)}, u32[]{:S(2)}) %collective-permute-start.20) | collective-permute-done | bytes 884768 | tf_op jit(solution)/shard_map/ppermute | solution.py:648
  139.3 1.6 add_convert_fusion
  141.0 3.8 %collective-permute-start.25 = (bf16[192,2304]{1,0:T(8,128)(2,1)S(1)}, bf16[192,2304]{1,0:T(8,128)(2,1)S(1)}, u32[]{:S(2)}, u32[]{:S(2)}) collective-permute-start(bf16[192,2304]{1,0:T(8,128)(2,1)S(1)} %add_convert_fusion), channel_id=1, source_target_pairs={{0,12},{1,13},{2,14},{3,15},{4,0},{5,1},{6,2},{7,3},{8,4},{9,5},{1... | collective-permute-start | bytes 2654216 | tf_op jit(solution)/shard_map/ppermute | solution.py:648
  144.7 1.8 %add_convert_fusion.1 = bf16[192,2304]{1,0:T(8,128)(2,1)S(1)} fusion(bf16[192,2304]{1,0:T(8,128)(2,1)} %collective-permute-done.20, bf16[192,2304]{1,0:T(8,128)(2,1)} %collective-permute-done.22, bf16[192,2304]{1,0:T(8,128)(2,1)S(1)} %copy-done.11), kind=kLoop, calls=%fused_computation.1 | loop fusion | flops 2654208 | bytes 3538944 | tf_op jit(solution)/shard_map/convert_element_type | solution.py:706
  146.6 4.0 %collective-permute-start.24 = (bf16[192,2304]{1,0:T(8,128)(2,1)S(1)}, bf16[192,2304]{1,0:T(8,128)(2,1)S(1)}, u32[]{:S(2)}, u32[]{:S(2)}) collective-permute-start(bf16[192,2304]{1,0:T(8,128)(2,1)S(1)} %add_convert_fusion.1), channel_id=1, source_target_pairs={{0,3},{1,0},{2,1},{3,2},{4,7},{5,4},{6,5},{7,6},{8,11},{9,8},{10,9... | collective-permute-start | bytes 2654216 | tf_op jit(solution)/shard_map/ppermute | solution.py:648
  150.6 2.7 %total.2 = bf16[192,2304]{1,0:T(8,128)(2,1)} custom-call(bf16[192,2304]{1,0:T(8,128)(2,1)S(1)} %copy-done.5, bf16[192,2304]{1,0:T(8,128)(2,1)S(1)} %collective-permute-done.17.refs_1_, bf16[192,2304]{1,0:T(8,128)(2,1)} %collective-permute-done.18.refs_2_, bf16[192,2304]{1,0:T(8,128)(2,1)S(1)} %collective-permute-done.19.refs_3_, bf16[384,384]{1,0:T(8,128)(2,1)S(1)} %copy-done), custom_call_target="tpu_custom_call" | custom-call | tf_op jit(solution)/shard_map/total/pallas_call | solution.py:626
  153.4 1.9 %collective-permute-done.25.refs_3_ = bf16[192,2304]{1,0:T(8,128)(2,1)S(1)} collective-permute-done((bf16[192,2304]{1,0:T(8,128)(2,1)S(1)}, bf16[192,2304]{1,0:T(8,128)(2,1)S(1)}, u32[]{:S(2)}, u32[]{:S(2)}) %collective-permute-start.25) | collective-permute-done | bytes 884768 | tf_op jit(solution)/shard_map/ppermute | solution.py:648
  155.3 5.9 %collective-permute-done.24.refs_2_ = bf16[192,2304]{1,0:T(8,128)(2,1)S(1)} collective-permute-done((bf16[192,2304]{1,0:T(8,128)(2,1)S(1)}, bf16[192,2304]{1,0:T(8,128)(2,1)S(1)}, u32[]{:S(2)}, u32[]{:S(2)}) %collective-permute-start.24) | collective-permute-done | bytes 884768 | tf_op jit(solution)/shard_map/ppermute | solution.py:648
  161.2 3.1 %collective-permute-done.23.refs_1_ = bf16[192,2304]{1,0:T(8,128)(2,1)S(1)} collective-permute-done((bf16[192,2304]{1,0:T(8,128)(2,1)S(1)}, bf16[192,2304]{1,0:T(8,128)(2,1)S(1)}, u32[]{:S(2)}, u32[]{:S(2)}) %collective-permute-start.23) | collective-permute-done | bytes 884768 | tf_op jit(solution)/shard_map/ppermute | solution.py:656
  164.3 1.7 %total.3 = bf16[192,2304]{1,0:T(8,128)(2,1)} custom-call(bf16[192,2304]{1,0:T(8,128)(2,1)S(1)} %copy-done.6, bf16[192,2304]{1,0:T(8,128)(2,1)S(1)} %collective-permute-done.23.refs_1_, bf16[192,2304]{1,0:T(8,128)(2,1)S(1)} %collective-permute-done.24.refs_2_, bf16[192,2304]{1,0:T(8,128)(2,1)S(1)} %collective-permute-done.25.refs_3_, bf16[384,384]{1,0:T(8,128)(2,1)S(1)} %copy-done), custom_call_target="tpu_custom_call" | custom-call | tf_op jit(solution)/shard_map/total/pallas_call | solution.py:626
  (80 shorter events, 4.1 us)
Async XLA Ops:
  0.6 13.4 %copy-start.16 = (s32[4,1]{0,1:T(1,128)S(1)}, s32[4,1]{0,1:T(1,128)}, u32[]{:S(2)}) copy-start(s32[4,1]{0,1:T(1,128)} %param.16) | copy-start | bytes 52
  0.6 13.4 %copy-start.17 = (s32[4]{0:T(128)S(1)}, s32[4]{0:T(128)}, u32[]{:S(2)}) copy-start(s32[4]{0:T(128)} %param.15) | copy-start | bytes 52
  0.7 13.4 %copy-start.15 = (s32[4]{0:T(128)S(1)}, s32[4]{0:T(128)}, u32[]{:S(2)}) copy-start(s32[4]{0:T(128)} %param.17) | copy-start | bytes 52
  0.7 1.0 copy-start.1
  1.6 1.2 copy-start.7
  2.8 9.6 %copy-start.14 = (s32[512,3]{0,1:T(4,128)S(1)}, s32[512,3]{0,1:T(4,128)}, u32[]{:S(2)}) copy-start(s32[512,3]{0,1:T(4,128)} %param.18) | copy-start | bytes 18436
  2.8 14.1 %copy-start.2 = (bf16[384,384]{1,0:T(8,128)(2,1)S(1)}, bf16[384,384]{1,0:T(8,128)(2,1)}, u32[]{:S(2)}) copy-start(bf16[384,384]{1,0:T(8,128)(2,1)} %constant.32.clone.refs_2_.refs_1_) | copy-start | bytes 884740
  2.8 14.1 %copy-start.4 = (bf16[4,48,2304]{2,1,0:T(8,128)(2,1)S(1)}, bf16[4,48,2304]{2,1,0:T(8,128)(2,1)}, u32[]{:S(2)}) copy-start(bf16[4,48,2304]{2,1,0:T(8,128)(2,1)} %param.13) | copy-start | bytes 2654212
  3.5 25.2 %copy-start.8 = (bf16[192,2304]{1,0:T(8,128)(2,1)}, bf16[192,2304]{1,0:T(8,128)(2,1)S(1)}, u32[]{:S(2)}) copy-start(bf16[192,2304]{1,0:T(8,128)(2,1)S(1)} %reorder.3.refs_9_) | copy-start | bytes 2654212
  3.5 15.3 %collective-permute-start = (bf16[192,2304]{1,0:T(8,128)(2,1)S(1)}, bf16[192,2304]{1,0:T(8,128)(2,1)}, u32[]{:S(2)}, u32[]{:S(2)}) collective-permute-start(bf16[192,2304]{1,0:T(8,128)(2,1)S(1)} %reorder.3.refs_9_), channel_id=1, source_target_pairs={{0,1},{1,2},{2,3},{3,0},{4,5},{5,6},{6,7},{7,4},{8,9},{9,10},{10,1... | collective-permute-start | bytes 2654216 | tf_op jit(solution)/shard_map/ppermute | solution.py:648
  5.6 14.4 %collective-permute-start.1 = (bf16[192,2304]{1,0:T(8,128)(2,1)S(1)}, bf16[192,2304]{1,0:T(8,128)(2,1)}, u32[]{:S(2)}, u32[]{:S(2)}) collective-permute-start(bf16[192,2304]{1,0:T(8,128)(2,1)S(1)} %reorder.3.refs_9_), channel_id=1, source_target_pairs={{0,4},{1,5},{2,6},{3,7},{4,8},{5,9},{6,10},{7,11},{8,12},{9,13},{1... | collective-permute-start | bytes 2654216 | tf_op jit(solution)/shard_map/ppermute | solution.py:648
  7.1 15.8 %collective-permute-start.2 = (bf16[192,2304]{1,0:T(8,128)(2,1)S(1)}, bf16[192,2304]{1,0:T(8,128)(2,1)S(1)}, u32[]{:S(2)}, u32[]{:S(2)}) collective-permute-start(bf16[192,2304]{1,0:T(8,128)(2,1)S(1)} %reorder.3.refs_9_), channel_id=1, source_target_pairs={{0,112},{16,0},{32,16},{48,32},{64,48},{80,64},{96,80},{112,96},{1... | collective-permute-start | bytes 2654216 | tf_op jit(solution)/shard_map/ppermute | solution.py:656
  17.7 26.7 %copy-start.3 = (bf16[208,2304]{1,0:T(8,128)(2,1)}, bf16[208,2304]{1,0:T(8,128)(2,1)S(1)}, u32[]{:S(2)}) copy-start(bf16[208,2304]{1,0:T(8,128)(2,1)S(1)} %reorder.2.refs_1_) | copy-start | bytes 2875396
  23.9 15.0 %collective-permute-start.3 = (bf16[208,2304]{1,0:T(8,128)(2,1)S(1)}, bf16[208,2304]{1,0:T(8,128)(2,1)S(1)}, u32[]{:S(2)}, u32[]{:S(2)}) collective-permute-start(bf16[208,2304]{1,0:T(8,128)(2,1)S(1)} %reorder.2.refs_1_), channel_id=1, source_target_pairs={{0,1},{1,2},{2,3},{3,0},{4,5},{5,6},{6,7},{7,4},{8,9},{9,10},{10,1... | collective-permute-start | bytes 2875400 | tf_op jit(solution)/shard_map/ppermute | solution.py:648
  23.9 15.0 %collective-permute-start.4 = (bf16[208,2304]{1,0:T(8,128)(2,1)S(1)}, bf16[208,2304]{1,0:T(8,128)(2,1)S(1)}, u32[]{:S(2)}, u32[]{:S(2)}) collective-permute-start(bf16[208,2304]{1,0:T(8,128)(2,1)S(1)} %reorder.2.refs_1_), channel_id=1, source_target_pairs={{0,4},{1,5},{2,6},{3,7},{4,8},{5,9},{6,10},{7,11},{8,12},{9,13},{1... | collective-permute-start | bytes 2875400 | tf_op jit(solution)/shard_map/ppermute | solution.py:648
  23.9 15.1 %collective-permute-start.5 = (bf16[208,2304]{1,0:T(8,128)(2,1)S(1)}, bf16[208,2304]{1,0:T(8,128)(2,1)}, u32[]{:S(2)}, u32[]{:S(2)}) collective-permute-start(bf16[208,2304]{1,0:T(8,128)(2,1)S(1)} %reorder.2.refs_1_), channel_id=1, source_target_pairs={{0,112},{16,0},{32,16},{48,32},{64,48},{80,64},{96,80},{112,96},{1... | collective-permute-start | bytes 2875400 | tf_op jit(solution)/shard_map/ppermute | solution.py:656
  38.9 19.0 %copy-start.13 = (bf16[208,2304]{1,0:T(8,128)(2,1)}, bf16[208,2304]{1,0:T(8,128)(2,1)S(1)}, u32[]{:S(2)}) copy-start(bf16[208,2304]{1,0:T(8,128)(2,1)S(1)} %collective-permute-done.3.refs_2_) | copy-start | bytes 2875396
  38.9 26.7 %copy-start.12 = (bf16[208,2304]{1,0:T(8,128)(2,1)}, bf16[208,2304]{1,0:T(8,128)(2,1)S(1)}, u32[]{:S(2)}) copy-start(bf16[208,2304]{1,0:T(8,128)(2,1)S(1)} %collective-permute-done.4.refs_3_) | copy-start | bytes 2875396
  39.0 18.9 %collective-permute-start.8 = (bf16[208,2304]{1,0:T(8,128)(2,1)S(1)}, bf16[208,2304]{1,0:T(8,128)(2,1)S(1)}, u32[]{:S(2)}, u32[]{:S(2)}) collective-permute-start(bf16[208,2304]{1,0:T(8,128)(2,1)S(1)} %collective-permute-done.4.refs_3_), channel_id=1, source_target_pairs={{0,3},{1,0},{2,1},{3,2},{4,7},{5,4},{6,5},{7,6},{8,11},{9,8},{10,9... | collective-permute-start | bytes 2875400 | tf_op jit(solution)/shard_map/ppermute | solution.py:648
  42.1 16.4 %collective-permute-start.9 = (bf16[208,2304]{1,0:T(8,128)(2,1)S(1)}, bf16[208,2304]{1,0:T(8,128)(2,1)S(1)}, u32[]{:S(2)}, u32[]{:S(2)}) collective-permute-start(bf16[208,2304]{1,0:T(8,128)(2,1)S(1)} %collective-permute-done.3.refs_2_), channel_id=1, source_target_pairs={{0,12},{1,13},{2,14},{3,15},{4,0},{5,1},{6,2},{7,3},{8,4},{9,5},{1... | collective-permute-start | bytes 2875400 | tf_op jit(solution)/shard_map/ppermute | solution.py:648
  42.2 15.2 %collective-permute-start.7 = (bf16[112,2304]{1,0:T(8,128)(2,1)S(1)}, bf16[112,2304]{1,0:T(8,128)(2,1)S(1)}, u32[]{:S(2)}, u32[]{:S(2)}) collective-permute-start(bf16[112,2304]{1,0:T(8,128)(2,1)S(1)} %slice.36), channel_id=1, source_target_pairs={{0,1},{1,2},{2,3},{3,0},{4,5},{5,6},{6,7},{7,4},{8,9},{9,10},{10,1... | collective-permute-start | bytes 1548296 | tf_op jit(solution)/shard_map/ppermute | solution.py:648
  42.3 14.4 %collective-permute-start.6 = (bf16[96,2304]{1,0:T(8,128)(2,1)S(1)}, bf16[96,2304]{1,0:T(8,128)(2,1)S(1)}, u32[]{:S(2)}, u32[]{:S(2)}) collective-permute-start(bf16[96,2304]{1,0:T(8,128)(2,1)S(1)} %slice.35), channel_id=1, source_target_pairs={{0,4},{1,5},{2,6},{3,7},{4,8},{5,9},{6,10},{7,11},{8,12},{9,13},{1... | collective-permute-start | bytes 1327112 | tf_op jit(solution)/shard_map/ppermute | solution.py:648
  56.7 1.9 %copy-start.23 = (bf16[96,2304]{1,0:T(8,128)(2,1)}, bf16[96,2304]{1,0:T(8,128)(2,1)S(1)}, u32[]{:S(2)}) copy-start(bf16[96,2304]{1,0:T(8,128)(2,1)S(1)} %collective-permute-done.6.refs_4_) | copy-start | bytes 1327108
  57.3 7.4 %copy-start.22 = (bf16[112,2304]{1,0:T(8,128)(2,1)}, bf16[112,2304]{1,0:T(8,128)(2,1)S(1)}, u32[]{:S(2)}) copy-start(bf16[112,2304]{1,0:T(8,128)(2,1)S(1)} %collective-permute-done.7.refs_5_) | copy-start | bytes 1548292
  57.9 0.9 copy-start.18
  58.6 1.0 copy-start.19
  60.3 27.5 %collective-permute-start.12 = (bf16[192,2304]{1,0:T(8,128)(2,1)}, bf16[192,2304]{1,0:T(8,128)(2,1)}, u32[]{:S(2)}, u32[]{:S(2)}) collective-permute-start(bf16[192,2304]{1,0:T(8,128)(2,1)} %collective-permute-done.1.refs_11_), channel_id=1, source_target_pairs={{0,3},{1,0},{2,1},{3,2},{4,7},{5,4},{6,5},{7,6},{8,11},{9,8},{10,9... | collective-permute-start | bytes 2654216 | tf_op jit(solution)/shard_map/ppermute | solution.py:648
  62.8 25.0 %collective-permute-start.13 = (bf16[192,2304]{1,0:T(8,128)(2,1)}, bf16[192,2304]{1,0:T(8,128)(2,1)}, u32[]{:S(2)}, u32[]{:S(2)}) collective-permute-start(bf16[192,2304]{1,0:T(8,128)(2,1)} %collective-permute-done.refs_10_), channel_id=1, source_target_pairs={{0,12},{1,13},{2,14},{3,15},{4,0},{5,1},{6,2},{7,3},{8,4},{9,5},{1... | collective-permute-start | bytes 2654216 | tf_op jit(solution)/shard_map/ppermute | solution.py:648
  64.3 23.2 %collective-permute-start.10 = (bf16[96,2304]{1,0:T(8,128)(2,1)S(1)}, bf16[96,2304]{1,0:T(8,128)(2,1)}, u32[]{:S(2)}, u32[]{:S(2)}) collective-permute-start(bf16[96,2304]{1,0:T(8,128)(2,1)S(1)} %slice.31), channel_id=1, source_target_pairs={{0,4},{1,5},{2,6},{3,7},{4,8},{5,9},{6,10},{7,11},{8,12},{9,13},{1... | collective-permute-start | bytes 1327112 | tf_op jit(solution)/shard_map/ppermute | solution.py:648
  64.8 22.7 %collective-permute-start.11 = (bf16[96,2304]{1,0:T(8,128)(2,1)S(1)}, bf16[96,2304]{1,0:T(8,128)(2,1)}, u32[]{:S(2)}, u32[]{:S(2)}) collective-permute-start(bf16[96,2304]{1,0:T(8,128)(2,1)S(1)} %slice.32), channel_id=1, source_target_pairs={{0,1},{1,2},{2,3},{3,0},{4,5},{5,6},{6,7},{7,4},{8,9},{9,10},{10,1... | collective-permute-start | bytes 1327112 | tf_op jit(solution)/shard_map/ppermute | solution.py:648
  77.6 25.3 %collective-permute-start.14 = (bf16[192,2304]{1,0:T(8,128)(2,1)}, bf16[192,2304]{1,0:T(8,128)(2,1)S(1)}, u32[]{:S(2)}, u32[]{:S(2)}) collective-permute-start(bf16[192,2304]{1,0:T(8,128)(2,1)} %get-tuple-element.83), channel_id=1, source_target_pairs={{0,12},{1,13},{2,14},{3,15},{4,0},{5,1},{6,2},{7,3},{8,4},{9,5},{1... | collective-permute-start | bytes 2654216 | tf_op jit(solution)/shard_map/ppermute | solution.py:648
  87.5 15.4 %collective-permute-start.15 = (bf16[192,2304]{1,0:T(8,128)(2,1)}, bf16[192,2304]{1,0:T(8,128)(2,1)}, u32[]{:S(2)}, u32[]{:S(2)}) collective-permute-start(bf16[192,2304]{1,0:T(8,128)(2,1)} %get-tuple-element.84), channel_id=1, source_target_pairs={{0,1},{1,2},{2,3},{3,0},{4,5},{5,6},{6,7},{7,4},{8,9},{9,10},{10,1... | collective-permute-start | bytes 2654216 | tf_op jit(solution)/shard_map/ppermute | solution.py:648
  87.5 15.5 %collective-permute-start.16 = (bf16[192,2304]{1,0:T(8,128)(2,1)}, bf16[192,2304]{1,0:T(8,128)(2,1)}, u32[]{:S(2)}, u32[]{:S(2)}) collective-permute-start(bf16[192,2304]{1,0:T(8,128)(2,1)} %get-tuple-element.85), channel_id=1, source_target_pairs={{0,4},{1,5},{2,6},{3,7},{4,8},{5,9},{6,10},{7,11},{8,12},{9,13},{1... | collective-permute-start | bytes 2654216 | tf_op jit(solution)/shard_map/ppermute | solution.py:648
  87.8 15.2 %collective-permute-start.17 = (bf16[192,2304]{1,0:T(8,128)(2,1)}, bf16[192,2304]{1,0:T(8,128)(2,1)S(1)}, u32[]{:S(2)}, u32[]{:S(2)}) collective-permute-start(bf16[192,2304]{1,0:T(8,128)(2,1)} %get-tuple-element.86), channel_id=1, source_target_pairs={{0,16},{16,32},{32,48},{48,64},{64,80},{80,96},{96,112},{112,0},{1... | collective-permute-start | bytes 2654216 | tf_op jit(solution)/shard_map/ppermute | solution.py:656
  102.9 6.6 %copy-start.9 = (bf16[192,2304]{1,0:T(8,128)(2,1)S(1)}, bf16[192,2304]{1,0:T(8,128)(2,1)}, u32[]{:S(2)}) copy-start(bf16[192,2304]{1,0:T(8,128)(2,1)} %get-tuple-element.117) | copy-start | bytes 2654212
  106.4 25.2 %collective-permute-start.19 = (bf16[192,2304]{1,0:T(8,128)(2,1)}, bf16[192,2304]{1,0:T(8,128)(2,1)S(1)}, u32[]{:S(2)}, u32[]{:S(2)}) collective-permute-start(bf16[192,2304]{1,0:T(8,128)(2,1)} %add_convert_fusion.2), channel_id=1, source_target_pairs={{0,12},{1,13},{2,14},{3,15},{4,0},{5,1},{6,2},{7,3},{8,4},{9,5},{1... | collective-permute-start | bytes 2654216 | tf_op jit(solution)/shard_map/ppermute | solution.py:648
  112.2 20.1 %collective-permute-start.18 = (bf16[192,2304]{1,0:T(8,128)(2,1)}, bf16[192,2304]{1,0:T(8,128)(2,1)}, u32[]{:S(2)}, u32[]{:S(2)}) collective-permute-start(bf16[192,2304]{1,0:T(8,128)(2,1)} %add_convert_fusion.3), channel_id=1, source_target_pairs={{0,3},{1,0},{2,1},{3,2},{4,7},{5,4},{6,5},{7,6},{8,11},{9,8},{10,9... | collective-permute-start | bytes 2654216 | tf_op jit(solution)/shard_map/ppermute | solution.py:648
  116.1 23.2 %collective-permute-start.20 = (bf16[192,2304]{1,0:T(8,128)(2,1)}, bf16[192,2304]{1,0:T(8,128)(2,1)}, u32[]{:S(2)}, u32[]{:S(2)}) collective-permute-start(bf16[192,2304]{1,0:T(8,128)(2,1)} %get-tuple-element.122), channel_id=1, source_target_pairs={{0,12},{1,13},{2,14},{3,15},{4,0},{5,1},{6,2},{7,3},{8,4},{9,5},{1... | collective-permute-start | bytes 2654216 | tf_op jit(solution)/shard_map/ppermute | solution.py:648
  116.1 23.2 %collective-permute-start.21 = (bf16[192,2304]{1,0:T(8,128)(2,1)}, bf16[192,2304]{1,0:T(8,128)(2,1)}, u32[]{:S(2)}, u32[]{:S(2)}) collective-permute-start(bf16[192,2304]{1,0:T(8,128)(2,1)} %get-tuple-element.123), channel_id=1, source_target_pairs={{0,1},{1,2},{2,3},{3,0},{4,5},{5,6},{6,7},{7,4},{8,9},{9,10},{10,1... | collective-permute-start | bytes 2654216 | tf_op jit(solution)/shard_map/ppermute | solution.py:648
  116.1 23.2 %collective-permute-start.22 = (bf16[192,2304]{1,0:T(8,128)(2,1)}, bf16[192,2304]{1,0:T(8,128)(2,1)}, u32[]{:S(2)}, u32[]{:S(2)}) collective-permute-start(bf16[192,2304]{1,0:T(8,128)(2,1)} %get-tuple-element.124), channel_id=1, source_target_pairs={{0,4},{1,5},{2,6},{3,7},{4,8},{5,9},{6,10},{7,11},{8,12},{9,13},{1... | collective-permute-start | bytes 2654216 | tf_op jit(solution)/shard_map/ppermute | solution.py:648
  131.6 13.2 %copy-start.11 = (bf16[192,2304]{1,0:T(8,128)(2,1)S(1)}, bf16[192,2304]{1,0:T(8,128)(2,1)}, u32[]{:S(2)}) copy-start(bf16[192,2304]{1,0:T(8,128)(2,1)} %get-tuple-element.129) | copy-start | bytes 2654212
  140.9 9.7 %copy-start.21 = (bf16[192,2304]{1,0:T(8,128)(2,1)S(1)}, bf16[192,2304]{1,0:T(8,128)(2,1)}, u32[]{:S(2)}) copy-start(bf16[192,2304]{1,0:T(8,128)(2,1)} %get-tuple-element.128) | copy-start | bytes 2654212
  141.0 9.6 %copy-start = (bf16[384,384]{1,0:T(8,128)(2,1)S(1)}, bf16[384,384]{1,0:T(8,128)(2,1)}, u32[]{:S(2)}) copy-start(bf16[384,384]{1,0:T(8,128)(2,1)} %constant.33.clone.refs_4_) | copy-start | bytes 884740
  141.0 9.6 %copy-start.5 = (bf16[192,2304]{1,0:T(8,128)(2,1)S(1)}, bf16[192,2304]{1,0:T(8,128)(2,1)}, u32[]{:S(2)}) copy-start(bf16[192,2304]{1,0:T(8,128)(2,1)} %get-tuple-element.107.refs_0_) | copy-start | bytes 2654212
  141.0 14.3 %collective-permute-start.25 = (bf16[192,2304]{1,0:T(8,128)(2,1)S(1)}, bf16[192,2304]{1,0:T(8,128)(2,1)S(1)}, u32[]{:S(2)}, u32[]{:S(2)}) collective-permute-start(bf16[192,2304]{1,0:T(8,128)(2,1)S(1)} %add_convert_fusion), channel_id=1, source_target_pairs={{0,12},{1,13},{2,14},{3,15},{4,0},{5,1},{6,2},{7,3},{8,4},{9,5},{1... | collective-permute-start | bytes 2654216 | tf_op jit(solution)/shard_map/ppermute | solution.py:648
  146.6 17.7 %copy-start.6 = (bf16[192,2304]{1,0:T(8,128)(2,1)S(1)}, bf16[192,2304]{1,0:T(8,128)(2,1)}, u32[]{:S(2)}) copy-start(bf16[192,2304]{1,0:T(8,128)(2,1)} %get-tuple-element.127.refs_0_) | copy-start | bytes 2654212
  146.6 14.6 %collective-permute-start.24 = (bf16[192,2304]{1,0:T(8,128)(2,1)S(1)}, bf16[192,2304]{1,0:T(8,128)(2,1)S(1)}, u32[]{:S(2)}, u32[]{:S(2)}) collective-permute-start(bf16[192,2304]{1,0:T(8,128)(2,1)S(1)} %add_convert_fusion.1), channel_id=1, source_target_pairs={{0,3},{1,0},{2,1},{3,2},{4,7},{5,4},{6,5},{7,6},{8,11},{9,8},{10,9... | collective-permute-start | bytes 2654216 | tf_op jit(solution)/shard_map/ppermute | solution.py:648
  150.6 13.7 %collective-permute-start.23 = (bf16[192,2304]{1,0:T(8,128)(2,1)S(1)}, bf16[192,2304]{1,0:T(8,128)(2,1)S(1)}, u32[]{:S(2)}, u32[]{:S(2)}) collective-permute-start(bf16[192,2304]{1,0:T(8,128)(2,1)S(1)} %copy-done.21), channel_id=1, source_target_pairs={{0,16},{16,32},{32,48},{48,64},{64,80},{80,96},{96,112},{112,0},{1... | collective-permute-start | bytes 2654216 | tf_op jit(solution)/shard_map/ppermute | solution.py:656
  (2 other events, 1.8 us)
